TPU v7x, 128 devices: a whole 4x4x4 slice. The times are simulated.
128 devices in a mesh: head: 8 (over y, core), expert: 16 (over z, x).
Axes of the slice: x: 4, y: 4, z: 4, core: 2. Of those that a mesh axis runs over, the one named last changes fastest.
Arguments:
- attention: bfloat16 [2048, 6144], P('expert', 'head'), may hold values from -6 to 6
- out_proj: bfloat16 [6144, 6144], P('head', 'expert'), may hold values from -0.078125 to 0.078125
- residual: bfloat16 [2048, 6144], P('expert', 'head'), may hold values from -64 to 64
- norm_gain: bfloat16 [6144], P('head'), may hold values from 0.25 to 1.75
- router: float32 [6144, 4], P('head'), may hold values from -0.02734375 to 0.02734375
- routes: int32 [2048, 2], P('expert'), may hold values from 0 to 3, all different within a row; in each aligned block of 128 rows (0 to 127, 128 to 255, ...) at most 72 rows name the same one
- cotangent: bfloat16 [2048, 6144], P('expert', 'head'), may hold values from -4 to 4
- gate_weight: bfloat16 [16, 6144, 2048], P('expert', None, 'head'), may hold values from -0.078125 to 0.078125
- up_weight: bfloat16 [16, 6144, 2048], P('expert', None, 'head'), may hold values from -0.078125 to 0.078125
- down_weight: bfloat16 [16, 2048, 6144], P('expert', None, 'head'), may hold values from -0.0625 to 0.0625
Outputs:
- layer_out: float32 [2048, 6144], P('expert', 'head')
- grad_gate: bfloat16 [16, 6144, 2048], P('expert', None, 'head')
- grad_up: bfloat16 [16, 6144, 2048], P('expert', None, 'head')
- grad_down: bfloat16 [16, 2048, 6144], P('expert', None, 'head')
Inputs may be any that keep to these rules, and one draw needn't show every extreme that they name: `routes`: each row names two different experts. In each aligned block of 128 rows (the rows of one index of expert) no expert is named by more than 72 rows, and in some block one expert is named by exactly 72 rows.
All inputs are finite; a program needn't handle non-finite values.
Results may differ from a plain program's by a relative error of at most 0.025.
Values may be sent and summed in bfloat16 or wider, within the bound.
A program may use at most 128 MiB of HBM per device.

v0:
```python
import jax
import jax.numpy as jnp
from jax import lax
from jax.sharding import PartitionSpec as P

EPSILON = 1e-05


def shards(
    attention,
    out_proj,
    residual,
    norm_gain,
    router,
    routes,
    cotangent,
    gate_weight,
    up_weight,
    down_weight,
):
    heads_count = lax.axis_size("head")
    owners = lax.axis_size("expert")
    tok_rows = attention.shape[0]
    experts_count = router.shape[1]
    group_size = owners // experts_count
    width = residual.shape[1] * heads_count
    capacity = tok_rows * 9 // 16
    contract_rows = (((0,), (0,)), ((), ()))
    partial_value = jnp.dot(
        attention,
        lax.all_gather(out_proj, "expert", axis=1, tiled=True),
        preferred_element_type=jnp.float32,
    )
    proj = lax.psum_scatter(
        partial_value.astype(jnp.bfloat16), "head", scatter_dimension=1, tiled=True
    ).astype(jnp.float32)
    state = residual.astype(jnp.float32) + proj
    scaled = state * norm_gain.astype(jnp.float32)
    square_sum = jnp.sum(state * state, axis=1)
    raw_logits = jnp.dot(
        scaled, router, precision=lax.Precision.HIGHEST, preferred_element_type=jnp.float32
    )
    total_square, logit_sum = lax.psum((square_sum, raw_logits), "head")
    inverse = lax.rsqrt(total_square / width + EPSILON)[:, None]
    normed = (scaled * inverse).astype(jnp.bfloat16)
    logits = inverse * logit_sum
    expert_ids = jnp.arange(experts_count, dtype=jnp.int32)
    first_id = routes[:, 0]
    second = routes[:, 1]
    logit_first = jnp.sum(
        jnp.where(first_id[:, None] == expert_ids[None, :], logits, 0.0), axis=1, keepdims=True
    )
    logit_second = jnp.sum(
        jnp.where(second[:, None] == expert_ids[None, :], logits, 0.0), axis=1, keepdims=True
    )
    prob_first = jax.nn.sigmoid(logit_first - logit_second)
    prob_second = jax.nn.sigmoid(logit_second - logit_first)
    flat_routes = routes.reshape(-1)
    hit_table = (flat_routes[:, None] == expert_ids[None, :]).astype(jnp.int32)
    earlier = jnp.cumsum(hit_table, axis=0, dtype=jnp.int32) - hit_table
    slot_pair = jnp.sum(earlier * hit_table, axis=1, dtype=jnp.int32).reshape(tok_rows, 2)
    buffer_rows = experts_count * capacity
    row_ids = jnp.arange(buffer_rows, dtype=jnp.int32)
    row_expert = row_ids // capacity
    row_slot = row_ids % capacity
    place_first = (
        (first_id[None, :] == row_expert[:, None]) & (slot_pair[:, 0][None, :] == row_slot[:, None])
    ).astype(jnp.bfloat16)
    place_second = (
        (second[None, :] == row_expert[:, None]) & (slot_pair[:, 1][None, :] == row_slot[:, None])
    ).astype(jnp.bfloat16)
    place_either = place_first + place_second
    features = lax.all_gather(normed, "head", axis=1, tiled=True)
    send_rows = jnp.dot(place_either, features, preferred_element_type=jnp.float32).astype(
        jnp.bfloat16
    )
    send_rows = send_rows.reshape(experts_count, capacity, features.shape[1])
    cot_first = (prob_first * cotangent.astype(jnp.float32)).astype(jnp.bfloat16)
    cot_second = (prob_second * cotangent.astype(jnp.float32)).astype(jnp.bfloat16)
    send_cot = jnp.dot(place_first, cot_first, preferred_element_type=jnp.float32) + jnp.dot(
        place_second, cot_second, preferred_element_type=jnp.float32
    )
    send_cot = send_cot.astype(jnp.bfloat16).reshape(experts_count, capacity, cotangent.shape[1])
    copies_rows = jnp.repeat(send_rows, group_size, axis=0)
    copies_cot = jnp.repeat(send_cot, group_size, axis=0)
    got_rows, got_cot = (
        lax.all_to_all(copies_rows, "expert", split_axis=0, concat_axis=0, tiled=True),
        lax.all_to_all(copies_cot, "expert", split_axis=0, concat_axis=0, tiled=True),
    )
    rows_total = owners * capacity
    x_rows = got_rows.reshape(rows_total, width)
    cot_rows = got_cot.reshape(rows_total, cotangent.shape[1])
    gate_w = gate_weight[0]
    up_w = up_weight[0]
    down_w = down_weight[0]
    gate_val = lax.dot_general(
        gate_w, x_rows, (((0,), (1,)), ((), ())), preferred_element_type=jnp.float32
    )
    up_val = lax.dot_general(
        up_w, x_rows, (((0,), (1,)), ((), ())), preferred_element_type=jnp.float32
    )
    act_gate = jax.nn.silu(gate_val)
    hidden_local = (act_gate * up_val).astype(jnp.bfloat16)
    hidden_all = lax.all_gather(hidden_local, "head", axis=0, tiled=True)
    partial_out = lax.dot_general(
        hidden_all, down_w, contract_rows, preferred_element_type=jnp.float32
    )
    partial_out = partial_out.reshape(owners, capacity, down_w.shape[1])
    returned = lax.all_to_all(
        partial_out.astype(jnp.bfloat16), "expert", split_axis=0, concat_axis=0, tiled=True
    ).astype(partial_out.dtype)
    slot_out = jnp.sum(
        returned.reshape(experts_count, group_size, capacity, down_w.shape[1]), axis=1
    )
    slot_out = slot_out.astype(jnp.bfloat16).reshape(buffer_rows, down_w.shape[1])
    took_first = lax.dot_general(
        place_first, slot_out, contract_rows, preferred_element_type=jnp.float32
    )
    took_second = lax.dot_general(
        place_second, slot_out, contract_rows, preferred_element_type=jnp.float32
    )
    layer_out = state + prob_first * took_first + prob_second * took_second
    grad_down = jnp.dot(hidden_all, cot_rows, preferred_element_type=jnp.float32).astype(
        jnp.bfloat16
    )
    hidden_grad = lax.psum_scatter(
        lax.dot_general(
            down_w, cot_rows, (((1,), (1,)), ((), ())), preferred_element_type=jnp.float32
        ).astype(jnp.bfloat16),
        "head",
        scatter_dimension=0,
        tiled=True,
    ).astype(jnp.float32)
    gate_sigmoid = jax.nn.sigmoid(gate_val)
    gate_grad = (
        hidden_grad * up_val * gate_sigmoid * (1.0 + gate_val * (1.0 - gate_sigmoid))
    ).astype(jnp.bfloat16)
    up_grad = (hidden_grad * act_gate).astype(jnp.bfloat16)
    grad_gate = lax.dot_general(
        x_rows, gate_grad, (((0,), (1,)), ((), ())), preferred_element_type=jnp.float32
    ).astype(jnp.bfloat16)
    grad_up = lax.dot_general(
        x_rows, up_grad, (((0,), (1,)), ((), ())), preferred_element_type=jnp.float32
    ).astype(jnp.bfloat16)
    return (layer_out, grad_gate[None], grad_up[None], grad_down[None])


def solution(mesh):
    return jax.shard_map(
        shards,
        mesh=mesh,
        in_specs=(
            P("expert", "head"),
            P("head", "expert"),
            P("expert", "head"),
            P("head"),
            P("head", None),
            P("expert", None),
            P("expert", "head"),
            P("expert", None, "head"),
            P("expert", None, "head"),
            P("expert", None, "head"),
        ),
        out_specs=(
            P("expert", "head"),
            P("expert", None, "head"),
            P("expert", None, "head"),
            P("expert", None, "head"),
        ),
        check_vma=False,
    )
```

profile of v0, /device:TPU:1, one launch (start us, length us, event | category | flops | bytes accessed | tf_op | source)
XLA Modules:
  0.0 525.8 jit_solution(8728416888221898792)
XLA Ops:
  7.2 0.7 all-gather.4.cloned.1.call-update
  8.0 88.3 %all-gather.4.cloned.1.call-done = bf16[768,6144]{1,0:T(8,128)(2,1)} async-done(((bf16[768,384]{1,0:T(8,128)(2,1)}), bf16[768,6144]{1,0:T(8,128)(2,1)}) %all-gather.4.cloned.1.call-update) | async-done | bytes 9437200 | tf_op jit(solution)/shard_map/all_gather | solution.py:31
  96.3 6.3 %convolution_convert_fusion.4 = bf16[128,6144]{1,0:T(8,128)(2,1)} fusion(bf16[128,768]{1,0:T(8,128)(2,1)} %param.10, bf16[768,6144]{1,0:T(8,128)(2,1)} %all-gather.4.cloned.1.call-done), kind=kOutput, calls=%fused_computation.6 | convolution fusion | flops 1208745984 | bytes 11206656 | tf_op jit(solution)/shard_map/dot_general | solution.py:29
  102.7 0.0 all-gather.6.cloned.1.call-start
  102.8 0.7 copy.20
  103.5 1.0 eq.128
  104.5 1.2 reduce-window.6
  105.7 0.1 slice.24
  105.8 0.1 copy.22
  105.9 0.6 slice.21
  106.5 0.8 copy.23
  107.3 25.5 %reduce-scatter.3.cloned.1.call-done = bf16[128,768]{1,0:T(8,128)(2,1)} async-done(((bf16[128,6144]{1,0:T(8,128)(2,1)}), bf16[128,768]{1,0:T(8,128)(2,1)}) %reduce-scatter.3.cloned.1.call-update) | async-done | bytes 196624 | tf_op jit(solution)/shard_map/reduce_scatter | solution.py:34
  132.8 1.6 multiply_reduce_fusion
  134.4 1.4 fusion.33
  135.7 16.1 %all-reduce = (f32[128]{0:T(128)}, f32[128,4]{0,1:T(4,128)}) all-reduce(f32[128]{0:T(128)} %multiply_reduce_fusion, f32[128,4]{0,1:T(4,128)S(1)} %fusion.33), channel_id=1, replica_groups=mesh['head'=8,'expert'=16] {'head'}, use_global_device_ids=true, to_apply=%region_2.0 | all-reduce | flops 640 | bytes 5120 | tf_op jit(solution)/shard_map/psum | solution.py:43
  151.8 0.7 add_rsqrt_fusion
  152.4 1.7 multiply_convert_fusion.1
  154.2 0.1 add_bitcast_fusion
  154.2 1.0 eq.124
  155.2 0.8 reshape.111
  156.0 1.1 slice_reduce_fusion.1
  157.1 0.8 slice_bitcast_fusion.1
  157.9 0.7 select_reduce_fusion.1
  158.6 0.4 fusion.37
  159.0 0.4 fusion.20
  159.4 1.3 broadcast_in_dim.17
  160.8 6.7 %all-to-all-start.2 = ((bf16[16,72,768]{2,1,0:T(8,128)(2,1)}), bf16[16,72,768]{2,1,0:T(8,128)(2,1)}, u32[]{:S(2)}, u32[]{:S(2)}) async-start(bf16[16,72,768]{2,1,0:T(8,128)(2,1)} %bitcast.83), calls=%async_computation.3 | async-start | bytes 3538944 | tf_op jit(solution)/shard_map/all_to_all | solution.py:88
  167.5 10.8 %all-gather.6.cloned.1.call-done = bf16[128,6144]{1,0:T(8,128)(2,1)} async-done(((bf16[128,768]{1,0:T(8,128)(2,1)}), bf16[128,6144]{1,0:T(8,128)(2,1)}) %all-gather.6.cloned.1.call-update) | async-done | bytes 1572880 | tf_op jit(solution)/shard_map/all_gather | solution.py:73
  178.2 4.3 convolution_convert_fusion
  182.6 9.7 %all-to-all-done.2 = bf16[16,72,768]{2,1,0:T(8,128)(2,1)} async-done(((bf16[16,72,768]{2,1,0:T(8,128)(2,1)}), bf16[16,72,768]{2,1,0:T(8,128)(2,1)}, u32[]{:S(2)}, u32[]{:S(2)}) %all-to-all-start.2) | async-done | bytes 1769504 | tf_op jit(solution)/shard_map/all_to_all | solution.py:88
  192.2 6.4 %broadcast_in_dim.16 = bf16[4,4,72,6144]{3,2,1,0:T(8,128)(2,1)} broadcast(bf16[4,72,6144]{2,1,0:T(8,128)(2,1)} %bitcast.82), dimensions={0,2,3} | broadcast | bytes 17694720 | tf_op jit(solution)/shard_map/broadcast_in_dim | solution.py:84
  198.6 5.2 all-to-all-start
  203.8 0.0 reduce-scatter.5.cloned.1.call-start
  203.9 7.0 %fusion.2 = bf16[2048,1152]{0,1:T(8,128)(2,1)} fusion(bf16[1152,768]{1,0:T(8,128)(2,1)} %bitcast.19, bf16[1,2048,768]{2,1,0:T(8,128)(2,1)S(1)} %copy-done), kind=kOutput, calls=%fused_computation.7 | convolution fusion | flops 3626237952 | bytes 9633792 | tf_op jit(solution)/shard_map/dot_general | solution.py:127
  210.9 0.0 all-gather.8.cloned.1.call-start
  210.9 195.5 %all-to-all-done = bf16[16,72,6144]{2,1,0:T(8,128)(2,1)} async-done(((bf16[16,72,6144]{2,1,0:T(8,128)(2,1)}), bf16[16,72,6144]{2,1,0:T(8,128)(2,1)}, u32[]{:S(2)}, u32[]{:S(2)}) %all-to-all-start) | async-done | bytes 14155808 | tf_op jit(solution)/shard_map/all_to_all | solution.py:87
  406.4 8.3 %fusion.11 = f32[256,1152]{0,1:T(8,128)S(1)} fusion(bf16[1152,6144]{1,0:T(8,128)(2,1)} %bitcast.6, bf16[1,6144,256]{2,1,0:T(8,128)(2,1)} %param.17), kind=kOutput, calls=%fused_computation.17 | convolution fusion | flops 3623878656 | bytes 18481152 | tf_op jit(solution)/shard_map/dot_general | solution.py:96
  414.7 10.7 %multiply_convert_fusion = (bf16[256,1152]{0,1:T(8,128)(2,1)}, f32[256,1152]{0,1:T(8,128)}) fusion(f32[256,1152]{0,1:T(8,128)S(1)} %fusion.11, bf16[1152,6144]{1,0:T(8,128)(2,1)} %bitcast.6, bf16[1,6144,256]{2,1,0:T(8,128)(2,1)S(1)} %copy-done.13), kind=kOutput, calls=%fused_computation.33 | convolution fusion | flops 3625648128 | bytes 20250624 | tf_op jit(solution)/shard_map/dot_general | solution.py:99
  425.5 12.1 %fusion = bf16[1,6144,256]{2,1,0:T(8,128)(2,1)} fusion(bf16[1152,6144]{1,0:T(8,128)(2,1)} %bitcast.6, f32[256,1152]{0,1:T(8,128)} %get-tuple-element.15, bf16[256,1152]{0,1:T(8,128)(2,1)} %reduce-scatter.5.cloned.1.call-done, f32[256,1152]{0,1:T(8,128)} %copy-done.14), kind=kOutput, calls=%fused_computation.4 | convolution fusion | flops 3628695552 | bytes 20250624 | tf_op jit(solution)/shard_map/dot_general | solution.py:139
  437.7 35.3 %all-gather.8.cloned.1.call-done = bf16[2048,1152]{0,1:T(8,128)(2,1)} async-done(((bf16[256,1152]{0,1:T(8,128)(2,1)}), bf16[2048,1152]{0,1:T(8,128)(2,1)}) %all-gather.8.cloned.1.call-update) | async-done | bytes 4718608 | tf_op jit(solution)/shard_map/all_gather | solution.py:104
  472.9 7.4 %fusion.17 = bf16[16,72,768]{2,1,0:T(8,128)(2,1)} fusion(bf16[16,72,2048]{2,1,0:T(8,128)(2,1)} %bitcast.88, bf16[1,2048,768]{2,1,0:T(8,128)(2,1)S(1)} %copy-done), kind=kOutput, calls=%fused_computation.20 | convolution fusion | flops 3624763392 | bytes 9633792 | tf_op jit(solution)/shard_map/dot_general | solution.py:105
  480.3 6.7 %all-to-all-start.1 = ((bf16[16,72,768]{2,1,0:T(8,128)(2,1)}), bf16[16,72,768]{2,1,0:T(8,128)(2,1)}, u32[]{:S(2)}, u32[]{:S(2)}) async-start(bf16[16,72,768]{2,1,0:T(8,128)(2,1)} %fusion.17), calls=%async_computation.2 | async-start | bytes 3538944 | tf_op jit(solution)/shard_map/all_to_all | solution.py:109
  487.1 11.8 %fusion.1 = bf16[1,6144,256]{2,1,0:T(8,128)(2,1)} fusion(bf16[1152,6144]{1,0:T(8,128)(2,1)} %bitcast.6, bf16[256,1152]{0,1:T(8,128)(2,1)} %reduce-scatter.5.cloned.1.call-done, f32[256,1152]{0,1:T(8,128)} %copy-done.14), kind=kOutput, calls=%fused_computation.5 | convolution fusion | flops 3627515904 | bytes 19070976 | tf_op jit(solution)/shard_map/dot_general | solution.py:142
  498.9 8.9 %fusion.10 = bf16[1,2048,768]{2,1,0:T(8,128)(2,1)} fusion(bf16[2048,1152]{0,1:T(8,128)(2,1)} %all-gather.8.cloned.1.call-done, bf16[1152,768]{1,0:T(8,128)(2,1)} %bitcast.19), kind=kOutput, calls=%fused_computation.16 | convolution fusion | flops 3625451520 | bytes 9633792 | tf_op jit(solution)/shard_map/dot_general | solution.py:123
  507.8 6.8 %all-to-all-done.1 = bf16[16,72,768]{2,1,0:T(8,128)(2,1)} async-done(((bf16[16,72,768]{2,1,0:T(8,128)(2,1)}), bf16[16,72,768]{2,1,0:T(8,128)(2,1)}, u32[]{:S(2)}, u32[]{:S(2)}) %all-to-all-start.1) | async-done | bytes 1769504 | tf_op jit(solution)/shard_map/all_to_all | solution.py:109
  514.6 1.7 bitcast_reduce_fusion
  516.3 1.1 convolution_multiply_fusion
  517.4 1.8 fusion.22
  (43 shorter events, 0.3 us)
Async XLA Ops:
  7.2 196.7 %copy-start = (bf16[1,2048,768]{2,1,0:T(8,128)(2,1)S(1)}, bf16[1,2048,768]{2,1,0:T(8,128)(2,1)}, u32[]{:S(2)}) copy-start(bf16[1,2048,768]{2,1,0:T(8,128)(2,1)} %param.19) | copy-start | bytes 9437188
  7.2 89.1 %all-gather.4.cloned.1.call-start = ((), (), s32[]{:S(2)}) async-start(), calls=%async_computation.5 | async-start | bytes 10027008 | tf_op jit(solution)/shard_map/all_gather | solution.py:31
  7.9 94.8 %copy-start.11 = (bf16[768]{0:T(1024)(128)(2,1)S(1)}, bf16[768]{0:T(1024)(128)(2,1)}, u32[]{:S(2)}) copy-start(bf16[768]{0:T(1024)(128)(2,1)} %param.13) | copy-start | bytes 4612
  7.9 94.8 %copy-start.10 = (s32[128,2]{0,1:T(2,128)S(1)}, s32[128,2]{0,1:T(2,128)}, u32[]{:S(2)}) copy-start(s32[128,2]{0,1:T(2,128)} %param.15) | copy-start | bytes 3076
  7.9 124.8 %copy-start.1 = (bf16[128,768]{1,0:T(8,128)(2,1)S(1)}, bf16[128,768]{1,0:T(8,128)(2,1)}, u32[]{:S(2)}) copy-start(bf16[128,768]{1,0:T(8,128)(2,1)} %param.12) | copy-start | bytes 589828
  7.9 124.8 %reduce-scatter.3.cloned.1.call-start = ((), (), s32[]{:S(2)}) async-start(), calls=%async_computation.6 | async-start | bytes 1769472 | tf_op jit(solution)/shard_map/reduce_scatter | solution.py:34
  102.7 56.0 %copy-start.3 = (bf16[128,768]{1,0:T(8,128)(2,1)S(1)}, bf16[128,768]{1,0:T(8,128)(2,1)}, u32[]{:S(2)}) copy-start(bf16[128,768]{1,0:T(8,128)(2,1)} %param.16) | copy-start | bytes 589828
  102.7 75.6 %all-gather.6.cloned.1.call-start = ((), (), s32[]{:S(2)}) async-start(), calls=%async_computation.7 | async-start | bytes 1769472 | tf_op jit(solution)/shard_map/all_gather | solution.py:73
  152.4 1.8 copy-start.12
  157.1 2.3 copy-start.4
  157.1 2.3 copy-start.6
  158.6 0.8 copy-start.8
  158.6 0.8 copy-start.9
  159.4 18.8 %copy-start.5 = (s32[128]{0:T(128)S(1)}, s32[128]{0:T(128)}, u32[]{:S(2)}) copy-start(s32[128]{0:T(128)} %copy-done.4) | copy-start | bytes 1540
  159.4 18.8 %copy-start.7 = (s32[128]{0:T(128)S(1)}, s32[128]{0:T(128)}, u32[]{:S(2)}) copy-start(s32[128]{0:T(128)} %copy-done.6) | copy-start | bytes 1540
  160.8 31.5 %all-to-all-start.2 = ((bf16[16,72,768]{2,1,0:T(8,128)(2,1)}), bf16[16,72,768]{2,1,0:T(8,128)(2,1)}, u32[]{:S(2)}, u32[]{:S(2)}) async-start(bf16[16,72,768]{2,1,0:T(8,128)(2,1)} %bitcast.83), calls=%async_computation.3 | async-start | bytes 3538944 | tf_op jit(solution)/shard_map/all_to_all | solution.py:88
  198.6 207.8 %all-to-all-start = ((bf16[16,72,6144]{2,1,0:T(8,128)(2,1)}), bf16[16,72,6144]{2,1,0:T(8,128)(2,1)}, u32[]{:S(2)}, u32[]{:S(2)}) async-start(bf16[16,72,6144]{2,1,0:T(8,128)(2,1)} %bitcast.81), calls=%async_computation.1 | async-start | bytes 28311552 | tf_op jit(solution)/shard_map/all_to_all | solution.py:87
  203.8 221.7 %reduce-scatter.5.cloned.1.call-start = ((), (), s32[]{:S(2)}) async-start(), calls=%async_computation.9 | async-start | bytes 5308416 | tf_op jit(solution)/shard_map/reduce_scatter | solution.py:126
  210.9 262.0 %all-gather.8.cloned.1.call-start = ((), (), s32[]{:S(2)}) async-start(), calls=%async_computation.8 | async-start | bytes 5308416 | tf_op jit(solution)/shard_map/all_gather | solution.py:104
  406.4 8.3 %copy-start.13 = (bf16[1,6144,256]{2,1,0:T(8,128)(2,1)S(1)}, bf16[1,6144,256]{2,1,0:T(8,128)(2,1)}, u32[]{:S(2)}) copy-start(bf16[1,6144,256]{2,1,0:T(8,128)(2,1)} %param.18) | copy-start | bytes 9437188
  414.7 10.7 %copy-start.14 = (f32[256,1152]{0,1:T(8,128)}, f32[256,1152]{0,1:T(8,128)S(1)}, u32[]{:S(2)}) copy-start(f32[256,1152]{0,1:T(8,128)S(1)} %fusion.11) | copy-start | bytes 3538948
  480.3 34.2 %all-to-all-start.1 = ((bf16[16,72,768]{2,1,0:T(8,128)(2,1)}), bf16[16,72,768]{2,1,0:T(8,128)(2,1)}, u32[]{:S(2)}, u32[]{:S(2)}) async-start(bf16[16,72,768]{2,1,0:T(8,128)(2,1)} %fusion.17), calls=%async_computation.2 | async-start | bytes 3538944 | tf_op jit(solution)/shard_map/all_to_all | solution.py:109
  507.8 9.6 %copy-start.2 = (bf16[128,768]{1,0:T(8,128)(2,1)S(1)}, bf16[128,768]{1,0:T(8,128)(2,1)}, u32[]{:S(2)}) copy-start(bf16[128,768]{1,0:T(8,128)(2,1)} %reduce-scatter.3.cloned.1.call-done) | copy-start | bytes 589828
Sparse Core Ops, SparseCore 0:
  10.1 86.1 all-gather.3
  102.8 29.9 reduce-scatter.2
  154.3 23.9 all-gather.5
  211.0 40.2 reduce-scatter.4
  425.6 47.2 all-gather.7
where the time goes:
time: 527 us; the launch traced here: 526 us
  waiting for transfers between devices  373 us (71%)
  matrix products  81.9 us (16%)
  starting transfers between devices  18.8 us (4%)
  blocking collectives  16.1 us (3%)
  local copies, waits for them, and re-layouts  14.6 us (3%)
  between operations  14.1 us (3%)
  other arithmetic  7.74 us (1%)
    all_to_all x1, waiting for transfers between devices, shards(): lax.all_to_all(copies_rows, 'expert', split_axis=0, concat_axis=0, tiled=...  195 us
    all_gather x1, waiting for transfers between devices, shards(): lax.all_gather(out_proj, 'expert', axis=1, tiled=True)  88.3 us
    all_gather x1, waiting for transfers between devices, shards(): hidden_all = lax.all_gather(hidden_local, 'head', axis=0, tiled=True)  35.3 us
    reduce_scatter x1, waiting for transfers between devices, shards(): lax.psum_scatter(partial_value.astype(jnp.bfloat16), 'head', scatter_dime...  25.5 us
    psum x1, blocking collectives, shards(): total_square, logit_sum = lax.psum((square_sum, raw_logits), 'head')  16.1 us
    dot_general x1, matrix products, shards(): lax.dot_general(x_rows, gate_grad, (((0,), (1,)), ((), ())), preferred_el...  12.1 us
    dot_general x1, matrix products, shards(): lax.dot_general(x_rows, up_grad, (((0,), (1,)), ((), ())), preferred_elem...  11.8 us
    all_gather x1, waiting for transfers between devices, shards(): features = lax.all_gather(normed, 'head', axis=1, tiled=True)  10.8 us
  transfers between devices with their start and end apart: 8, of which 7 were waited for; matrix products, arithmetic and copies ran while one was open for 14% of the time, Pallas kernels for 0%

commit v1 on v0

v1 whole, which is shorter than its diff:
```python
import functools

import jax
import jax.numpy as jnp
from jax import lax
from jax.experimental import pallas as pl
from jax.experimental.pallas import tpu as pltpu
from jax.sharding import PartitionSpec as P

EPSILON = 1e-05
MESH = pl.DeviceIdType.MESH
BF = jnp.bfloat16
F32 = jnp.float32
MIB = 2**20


def coords():
    e, h = lax.axis_index("expert"), lax.axis_index("head")
    return e % 4, h // 2, e // 4, h % 2


def dev(x, y, z, c):
    return {"expert": z * 4 + x, "head": 2 * y + c}


def rot(i, k):
    return lax.rem(i + (k + 4), 4)


def contract(a, b, ca, cb, **kw):
    return lax.dot_general(
        a, b, (((ca,), (cb,)), ((), ())), preferred_element_type=F32, **kw
    )


class Net:
    def __init__(self, ssem, rsem, mate):
        self.ssem, self.rsem, self.mate = ssem, rsem, mate
        self.n, self.sent = 0, []

    def send(self, src, dst, to):
        tag = self.n
        self.n += 1
        copy = pltpu.make_async_remote_copy(
            src_ref=src,
            dst_ref=dst,
            send_sem=self.ssem.at[tag],
            recv_sem=self.rsem.at[tag],
            device_id=to,
            device_id_type=MESH,
        )
        copy.start()
        self.sent.append(copy)
        return tag

    def wait(self, tag, dst):
        pltpu.make_async_remote_copy(
            src_ref=dst,
            dst_ref=dst,
            send_sem=self.ssem.at[tag],
            recv_sem=self.rsem.at[tag],
            device_id=self.mate,
            device_id_type=MESH,
        ).wait_recv()

    def drain(self):
        for copy in self.sent:
            copy.wait_send()
        self.sent = []


class Gather:
    def __init__(self, net, at, a, b, to_a, to_b, lo, hi, share):
        self.net, self.at, self.a, self.b = net, at, a, b
        self.to_a, self.to_b, self.lo, self.hi, self.share = to_a, to_b, lo, hi, share
        self.t = {}

    def ref(self, ka, kb):
        return self.at(rot(self.a, ka), rot(self.b, kb))

    def along_b(self, ka):
        r = self.ref(ka, 0)
        self.t[ka, -1] = self.net.send(r, r, self.to_b(1))
        self.t[ka, 1] = self.net.send(r, r, self.to_b(-1))

    def begin(self):
        r = self.ref(0, 0)
        self.t["a", -1] = self.net.send(r, r, self.to_a(1))
        self.t["a", 1] = self.net.send(r, r, self.to_a(-1))
        self.along_b(0)
        self.share(0, 0)

    def near_a(self):
        for k, part in ((-1, self.lo), (1, self.hi)):
            r = self.ref(k, 0)
            self.net.wait(self.t["a", k], r)
            self.t["f", k] = self.net.send(r.at[part], r.at[part], self.to_a(-k))
            self.along_b(k)
            self.share(k, 0)

    def far_a(self):
        r = self.ref(2, 0)
        self.net.wait(self.t["f", -1], r.at[self.lo])
        self.net.wait(self.t["f", 1], r.at[self.hi])
        self.along_b(2)
        self.share(2, 0)

    def near_b(self, ka):
        for k, part in ((-1, self.lo), (1, self.hi)):
            r = self.ref(ka, k)
            self.net.wait(self.t[ka, k], r)
            self.t["f", ka, k] = self.net.send(r.at[part], r.at[part], self.to_b(-k))
            self.share(ka, k)

    def far_b(self, ka):
        r = self.ref(ka, 2)
        self.net.wait(self.t["f", ka, -1], r.at[self.lo])
        self.net.wait(self.t["f", ka, 1], r.at[self.hi])
        self.share(ka, 2)


def greet(devices, extra=()):
    barrier = pltpu.get_barrier_semaphore()
    for d in devices:
        pl.semaphore_signal(barrier, inc=1, device_id=d, device_id_type=MESH)
    count = len(devices)
    for d, mine in extra:

        @pl.when(jnp.logical_not(mine))
        def _(d=d):
            pl.semaphore_signal(barrier, inc=1, device_id=d, device_id_type=MESH)

        count = count + jnp.where(mine, 0, 1)
    pl.semaphore_wait(barrier, count)


def slot_masks(rts_ref, capacity):
    r0, r1 = rts_ref[0:1, :], rts_ref[1:2, :]
    n = r0.shape[1]
    ids = lax.broadcasted_iota(jnp.int32, (8, n), 0)
    hits = ((r0 == ids) | (r1 == ids)).astype(F32).astype(BF)
    before = (
        lax.broadcasted_iota(jnp.int32, (n, n), 0)
        < lax.broadcasted_iota(jnp.int32, (n, n), 1)
    ).astype(F32).astype(BF)
    earlier = contract(hits, before, 1, 0)
    slot0 = jnp.sum(jnp.where(r0 == ids, earlier, 0.0), axis=0, keepdims=True)
    slot1 = jnp.sum(jnp.where(r1 == ids, earlier, 0.0), axis=0, keepdims=True)
    rows = lax.broadcasted_iota(jnp.int32, (capacity, n), 0)
    slot0, slot1 = slot0.astype(jnp.int32), slot1.astype(jnp.int32)
    return [
        ((r0 == e) & (slot0 == rows), (r1 == e) & (slot1 == rows)) for e in range(4)
    ]


def as_column(row):
    n = row.shape[1]
    eye = lax.broadcasted_iota(jnp.int32, (n, n), 0) == lax.broadcasted_iota(
        jnp.int32, (n, n), 1
    )
    return jnp.sum(jnp.where(eye, row, 0.0), axis=1, keepdims=True)


def front_kernel(
    att, op, res, gain, rt, rts, cot,
    state_o, xs_o, cs_o, pr_o,
    attb, own, sib16, sibr, r1, fin, st2, tot16, projr, stat, xrow, crow, xr, cr,
    ssem, rsem, lsem,
):
    x, y, z, c = coords()
    h = lax.axis_index("head")
    mate = dev(x, y, z, 1 - c)
    net = Net(ssem, rsem, mate)
    turn = [(dev(2 * c + j, z, y, x // 2), (x == 2 * c + j) & (y == z) & (c == x // 2)) for j in range(2)]
    group = [
        {"expert": lax.axis_index("expert"), "head": lax.rem(h + k, 8)}
        for k in range(1, 8)
    ]
    greet(
        [dev(rot(x, 1), y, z, c), dev(rot(x, -1), y, z, c)]
        + [dev(x, y, rot(z, k), c) for k in (1, 2, 3)]
        + group,
        turn,
    )
    attb[z, x] = att[...].reshape(attb.shape[2:])

    def quiet(ka, kb):
        pass

    lo, hi = pl.ds(0, 32), pl.ds(32, 32)
    g0 = Gather(net, lambda a, b: attb.at[b, a, 0], x, z, lambda k: dev(rot(x, k), y, z, c), lambda k: dev(x, y, rot(z, k), c), lo, hi, quiet)
    g1 = Gather(net, lambda a, b: attb.at[a, b, 1], z, x, lambda k: dev(x, y, rot(z, k), c), lambda k: dev(rot(x, k), y, z, c), lo, hi, quiet)
    flows = (g0, g1)
    for g in flows:
        g.begin()
    capacity = xrow.shape[1]
    masks = slot_masks(rts, capacity)
    for e, (m0, m1) in enumerate(masks):
        pick = (m0 | m1).astype(F32).astype(BF)
        crow[e] = contract(pick, cot[...], 1, 0).astype(BF)
    for g in flows:
        g.near_a()
    for g in flows:
        g.near_b(0)
    for g in flows:
        g.far_a()
    for k in (-1, 1):
        for g in flows:
            g.near_b(k)
    for k in (0, -1):
        for g in flows:
            g.far_b(k)
    for g in flows:
        g.near_b(2)
    for k in (1, 2):
        for g in flows:
            g.far_b(k)

    def product(yy, cc):
        rows = attb[yy, pl.ds(2 * cc, 2)].reshape(256, att.shape[1])
        return contract(rows, op[...], 1, 0)

    tags = {}
    for k in (2, -1, 1, 0):
        yy = rot(y, k)
        sib16[yy] = product(yy, 1 - c).astype(BF)
        tags[k] = net.send(sib16.at[yy], sibr.at[yy], mate)
    for k in (2, -1, 1, 0):
        yy = rot(y, k)
        own[yy] = product(yy, c)
    for k in (2, -1, 1, 0):
        yy = rot(y, k)
        net.wait(tags[k], sibr.at[yy])
        own[yy] += sibr[yy].astype(F32)
        if k == 2:
            st2[0] = own[yy].astype(BF)
            ta = net.send(st2.at[0, pl.ds(0, 128)], r1.at[0], dev(x, rot(y, 1), z, c))
            tb = net.send(
                st2.at[0, pl.ds(128, 128)], r1.at[1], dev(x, rot(y, -1), z, c)
            )
    net.wait(ta, r1.at[0])
    yy = rot(y, 1)
    own[yy, 0:128, :] += r1[0].astype(F32)
    st2[1] = own[yy].astype(BF)
    tc = net.send(st2.at[1], fin.at[0], dev(x, yy, z, c))
    net.wait(tb, r1.at[1])
    yy = rot(y, -1)
    own[yy, 128:256, :] += r1[1].astype(F32)
    st2[2] = own[yy].astype(BF)
    td = net.send(st2.at[2], fin.at[1], dev(x, yy, z, c))
    net.wait(tc, fin.at[0])
    net.wait(td, fin.at[1])
    total = own[y] + fin[0].astype(F32) + fin[1].astype(F32)
    tot16[...] = total.reshape(tot16.shape).astype(BF)

    base = net.n
    net.n += 2
    i = x % 2
    for j, (d, mine) in enumerate(turn):

        def remote(j=j, d=d):
            return pltpu.make_async_remote_copy(
                src_ref=tot16.at[j],
                dst_ref=projr.at[i],
                send_sem=ssem.at[base + j],
                recv_sem=rsem.at[base + i],
                device_id=d,
                device_id_type=MESH,
            )

        @pl.when(mine)
        def _(j=j):
            pltpu.make_async_copy(tot16.at[j], projr.at[i], lsem.at[0]).start()

        @pl.when(jnp.logical_not(mine))
        def _(remote=remote):
            remote().start()

    for k in range(2):
        local = (x == 2 * c + k) & (y == z) & (c == x // 2)

        @pl.when(local)
        def _(k=k):
            pltpu.make_async_copy(tot16.at[0], projr.at[k], lsem.at[0]).wait()

        @pl.when(jnp.logical_not(local))
        def _(k=k):
            net.wait(base + k, projr.at[k])

    for j, (d, mine) in enumerate(turn):

        @pl.when(jnp.logical_not(mine))
        def _(j=j, d=d):
            pltpu.make_async_remote_copy(
                src_ref=tot16.at[j],
                dst_ref=projr.at[i],
                send_sem=ssem.at[base + j],
                recv_sem=rsem.at[base + i],
                device_id=d,
                device_id_type=MESH,
            ).wait_send()

    half = projr.shape[2]
    for k in range(2):
        cols = slice(k * half, (k + 1) * half)
        state_o[:, cols] = res[:, cols].astype(F32) + projr[k].astype(F32)
    state = state_o[...]
    scaled = state * gain[...].astype(F32)
    stat[h, 0:4, :] = contract(rt[...], scaled, 1, 1, precision=lax.Precision.HIGHEST)
    ones = jnp.ones((8, state.shape[1]), F32)
    squares = contract(ones, state * state, 1, 1, precision=lax.Precision.HIGHEST)
    stat[h, 4:8, :] = squares[0:4]
    tags = [net.send(stat.at[h], stat.at[h], d) for d in group]
    for k, tag in enumerate(tags):
        net.wait(tag, stat.at[lax.rem(h + 7 - k, 8)])
    sums = stat[0]
    for k in range(1, 8):
        sums = sums + stat[k]
    width = 8.0 * state.shape[1]
    inverse = lax.rsqrt(sums[4:5] / width + EPSILON)
    logits = sums[0:4] * inverse
    ids = lax.broadcasted_iota(jnp.int32, logits.shape, 0)
    l0 = jnp.sum(jnp.where(rts[0:1, :] == ids, logits, 0.0), axis=0, keepdims=True)
    l1 = jnp.sum(jnp.where(rts[1:2, :] == ids, logits, 0.0), axis=0, keepdims=True)
    p0, p1 = jax.nn.sigmoid(l0 - l1), jax.nn.sigmoid(l1 - l0)
    pr_o[0:1, :] = p0
    pr_o[1:2, :] = p1
    normed = (scaled * as_column(inverse)).astype(BF)
    for e, (m0, m1) in enumerate(masks):
        pick = (m0 | m1).astype(F32).astype(BF)
        xrow[e] = contract(pick, normed, 1, 0).astype(BF)
    moved = []
    for k in (1, 2, 3):
        e = rot(z, k)
        tag = net.send(xrow.at[e], xr.at[z], dev(x, y, e, c))
        moved.append((tag, xr.at[rot(z, -k)]))
    for e, (m0, m1) in enumerate(masks):
        share = jnp.sum(
            jnp.where(m0, p0, 0.0) + jnp.where(m1, p1, 0.0), axis=1, keepdims=True
        )
        crow[e] = (crow[e].astype(F32) * share).astype(BF)
    for k in (1, 2, 3):
        e = rot(z, k)
        tag = net.send(crow.at[e], cr.at[z], dev(x, y, e, c))
        moved.append((tag, cr.at[rot(z, -k)]))
    xr[z] = xrow[z]
    cr[z] = crow[z]
    for tag, ref in moved:
        net.wait(tag, ref)
    xs_o[...] = xr[...]
    cs_o[...] = cr[...]
    net.drain()


def front(attention, out_proj, residual, norm_gain, router, routes, cotangent):
    vmem = pl.BlockSpec(memory_space=pltpu.VMEM)
    rows, cols = attention.shape
    width = out_proj.shape[1]
    cap = rows * 9 // 16
    sds = jax.ShapeDtypeStruct
    return pl.pallas_call(
        front_kernel,
        out_shape=(
            sds((rows, cols), F32),
            sds((4, cap, cols), BF),
            sds((4, cap, cols), BF),
            sds((8, rows), F32),
        ),
        in_specs=[vmem] * 7,
        out_specs=(vmem,) * 4,
        scratch_shapes=[
            pltpu.VMEM((4, 4, 2, rows // 2, cols), BF),
            pltpu.VMEM((4, 2 * rows, width), F32),
            pltpu.VMEM((4, 2 * rows, width), BF),
            pltpu.VMEM((4, 2 * rows, width), BF),
            pltpu.VMEM((2, rows, width), BF),
            pltpu.VMEM((2, 2 * rows, width), BF),
            pltpu.VMEM((3, 2 * rows, width), BF),
            pltpu.VMEM((2, rows, width), BF),
            pltpu.VMEM((2, rows, width), BF),
            pltpu.VMEM((8, 8, rows), F32),
            pltpu.VMEM((4, cap, cols), BF),
            pltpu.VMEM((4, cap, cols), BF),
            pltpu.VMEM((4, cap, cols), BF),
            pltpu.VMEM((4, cap, cols), BF),
            pltpu.SemaphoreType.DMA((64,)),
            pltpu.SemaphoreType.DMA((64,)),
            pltpu.SemaphoreType.DMA((1,)),
        ],
        compiler_params=pltpu.CompilerParams(
            collective_id=0, has_side_effects=True, vmem_limit_bytes=40 * MIB
        ),
        cost_estimate=pl.CostEstimate(
            flops=3_000_000_000, bytes_accessed=4_000_000, transcendentals=0
        ),
    )(
        attention,
        out_proj,
        residual,
        norm_gain[None, :],
        router.T,
        routes.T,
        cotangent,
    )


def shards(attention, out_proj, residual, norm_gain, router, routes, cotangent, gate_weight, up_weight, down_weight):
    state, xs, cs, pr = front(attention, out_proj, residual, norm_gain, router, routes, cotangent)
    groups = [[4 * z + x for x in range(4)] for z in range(4)]
    xg = lax.all_gather(xs, "expert", axis=0, tiled=True, axis_index_groups=groups)
    cg = lax.all_gather(cs, "expert", axis=0, tiled=True, axis_index_groups=groups)
    x_rows = lax.all_gather(xg, "head", axis=2, tiled=True).reshape(1152, 6144)
    cot_rows = cg.reshape(1152, 768)
    gate_w = gate_weight[0]; up_w = up_weight[0]; down_w = down_weight[0]
    g = contract(x_rows, gate_w, 1, 0); u = contract(x_rows, up_w, 1, 0)
    act = jax.nn.silu(g)
    hid = (act * u).astype(BF)
    hid_all = lax.all_gather(hid, "head", axis=1, tiled=True)
    yp = contract(hid_all, down_w, 1, 0).astype(BF)
    yp = yp.reshape(4, 4, 72, 768).transpose(1, 0, 2, 3).reshape(16, 72, 768)
    ret = lax.all_to_all(yp, "expert", split_axis=0, concat_axis=0, tiled=True).astype(F32)
    slot_out = jnp.sum(ret.reshape(4, 4, 72, 768), axis=1).astype(BF).reshape(288, 768)
    grad_down = contract(hid_all, cot_rows, 0, 0).astype(BF)
    dh = lax.psum_scatter(contract(cot_rows, down_w, 1, 1).astype(BF), "head", scatter_dimension=1, tiled=True).astype(F32)
    s = jax.nn.sigmoid(g)
    da = (dh * u * s * (1.0 + g * (1.0 - s))).astype(BF)
    db = (dh * act).astype(BF)
    gg = contract(x_rows, da, 0, 0).astype(BF); gu = contract(x_rows, db, 0, 0).astype(BF)
    r0, r1 = routes[:, 0], routes[:, 1]
    ids = jnp.arange(4)
    hits = ((r0[:, None] == ids) | (r1[:, None] == ids)).astype(F32)
    earlier = jnp.dot(jnp.tril(jnp.ones((128, 128), F32), -1), hits)
    s0 = jnp.sum(jnp.where(r0[:, None] == ids, earlier, 0), axis=1).astype(jnp.int32) + r0 * 72
    s1 = jnp.sum(jnp.where(r1[:, None] == ids, earlier, 0), axis=1).astype(jnp.int32) + r1 * 72
    rid = jnp.arange(288)
    t0 = jnp.dot((s0[:, None] == rid).astype(BF), slot_out, preferred_element_type=F32)
    t1 = jnp.dot((s1[:, None] == rid).astype(BF), slot_out, preferred_element_type=F32)
    out = state + pr[0][:, None] * t0 + pr[1][:, None] * t1
    return out, gg[None], gu[None], grad_down[None]


def solution(mesh):
    token = P("expert", "head")
    weight = P("expert", None, "head")
    return jax.shard_map(
        shards,
        mesh=mesh,
        in_specs=(token, P("head", "expert"), token, P("head"), P("head", None), P("expert", None), token)
        + (weight,) * 3,
        out_specs=(token,) + (weight,) * 3,
        check_vma=False,
    )
```

time: 527 us -> 351 us (0.67)
  waiting for transfers between devices: 373 us -> 184 us
  Pallas kernels: 0 us -> 71.6 us
  matrix products: 81.9 us -> 61 us
  blocking collectives: 16.1 us -> 0 us
  starting transfers between devices: 18.8 us -> 6.92 us
  other arithmetic: 7.74 us -> 1.73 us
    all_to_all x3 -> x1, waiting for transfers between devices: 212 us -> 7.49 us  [shards(): lax.all_to_all(yp, 'expert', split_axis=0, concat_axis=0, tiled=True)]
    pallas_call x0 -> x1, Pallas kernels: none -> 71.6 us  [front(): pl.pallas_call(front_kernel, out_shape=(sds((rows, cols), F32), sds((4, c...]
    dot_general x14 -> x10, matrix products: 81.9 us -> 61 us  [the longest x7 59.4 us: contract(): lax.dot_general(a, b, (((ca,), (cb,)), ((), ())), preferred_element_type=...]
    all_gather x3 -> x4, waiting for transfers between devices: 134 us -> 154 us  [the longest x1 68.9 us: shards(): x_rows = lax.all_gather(xg, 'head', axis=2, tiled=True).reshape(1152, 6144)]
    psum x1 -> x0, blocking collectives: 16.1 us -> none  [shards(): total_square, logit_sum = lax.psum((square_sum, raw_logits), 'head')]
    all_to_all x3 -> x1, starting transfers between devices: 18.6 us -> 6.72 us  [shards(): lax.all_to_all(yp, 'expert', split_axis=0, concat_axis=0, tiled=True)]
    unnamed x31 -> x30, local copies, waits for them, and re-layouts: 0.81 us -> 8.92 us
    broadcast_in_dim x2 -> x1, local copies, waits for them, and re-layouts: 7.72 us -> 0.84 us  [front(): norm_gain[None, :]]
  transfers between devices with their start and end apart: 8 -> 6, of which waited for: 7 -> 6; matrix products, arithmetic and copies ran while one was open for 14% -> 15% of each run, Pallas kernels for 0% -> 0%
where the time goes in v1:
time: 351 us; the launch traced here: 350 us
  waiting for transfers between devices  184 us (52%)
  Pallas kernels  71.6 us (20%)
  matrix products  61 us (17%)
  between operations  13.9 us (4%)
  local copies, waits for them, and re-layouts  11.6 us (3%)
  starting transfers between devices  6.92 us (2%)
    pallas_call x1, Pallas kernels, front(): pl.pallas_call(front_kernel, out_shape=(sds((rows, cols), F32), sds((4, c...  71.6 us
    all_gather x1, waiting for transfers between devices, shards(): x_rows = lax.all_gather(xg, 'head', axis=2, tiled=True).reshape(1152, 6144)  68.9 us
    dot_general x7, matrix products, contract(): lax.dot_general(a, b, (((ca,), (cb,)), ((), ())), preferred_element_type=...  59.4 us
    all_gather x1, waiting for transfers between devices, shards(): hid_all = lax.all_gather(hid, 'head', axis=1, tiled=True)  30.7 us
    all_gather x1, waiting for transfers between devices, shards(): lax.all_gather(cs, 'expert', axis=0, tiled=True, axis_index_groups=groups)  30.3 us
    all_gather x1, waiting for transfers between devices, shards(): lax.all_gather(xs, 'expert', axis=0, tiled=True, axis_index_groups=groups)  24 us
    reduce_scatter x1, waiting for transfers between devices, shards(): lax.psum_scatter(contract(cot_rows, down_w, 1, 1).astype(BF), 'head', sca...  21.5 us
    unnamed x30, local copies, waits for them, and re-layouts  8.92 us
  transfers between devices with their start and end apart: 6, of which 6 were waited for; matrix products, arithmetic and copies ran while one was open for 15% of the time, Pallas kernels for 0%

profile of v1, /device:TPU:1, one launch (start us, length us, event | category | flops | bytes accessed | tf_op | source)
XLA Modules:
  0.0 350.4 jit_solution(13019541387778320548)
XLA Ops:
  7.2 0.0 copy-start
  7.2 0.0 all-gather.5.cloned.1.call-start
  7.2 0.8 broadcast_in_dim.32.gain
  8.1 0.7 copy-done.3
  8.8 1.1 copy-done.5
  9.9 0.9 copy-done.6
  10.8 0.9 copy-done.7
  11.7 0.9 copy-done.8
  12.7 0.7 copy-done.9
  13.4 71.6 %shard_map.129 = (f32[128,768]{1,0:T(8,128)S(1)}, bf16[4,72,768]{2,1,0:T(8,128)(2,1)S(1)}, bf16[4,72,768]{2,1,0:T(8,128)(2,1)S(1)}, f32[8,128]{1,0:T(8,128)S(1)}) custom-call(bf16[128,768]{1,0:T(8,128)(2,1)S(1)} %copy-done.6, bf16[768,384]{1,0:T(8,128)(2,1)S(1)} %copy-done.5, bf16[128,768]{1,0:T(8,128)(2,1)S(1)} %copy-done.7, ...), custom_call_target="tpu_custom_call" | custom-call | flops 3000000000 | bytes 4000000 | tf_op jit(solution)/shard_map/pallas_call | solution.py:361
  85.0 0.0 copy-start.1
  85.0 0.8 copy-done.1
  85.7 0.8 copy-done.2
  86.5 0.0 all-gather.5.cloned.1.call-update
  86.5 0.0 all-gather.11.cloned.1.call-start
  86.6 0.7 all-gather.11.cloned.1.call-update
  87.3 0.0 all-gather.7.cloned.1.call-start
  87.3 24.0 %all-gather.5.cloned.1.call-done = bf16[16,72,768]{2,1,0:T(8,128)(2,1)} async-done(((bf16[4,72,768]{2,1,0:T(8,128)(2,1)}), bf16[16,72,768]{2,1,0:T(8,128)(2,1)}) %all-gather.5.cloned.1.call-update) | async-done | bytes 1769488 | tf_op jit(solution)/shard_map/all_gather | solution.py:410
  111.3 0.0 all-gather.7.cloned.1.call-update
  111.3 0.0 reduce-scatter.2.cloned.1.call-start
  111.3 30.3 %all-gather.11.cloned.1.call-done = bf16[16,72,768]{2,1,0:T(8,128)(2,1)} async-done(((bf16[4,72,768]{2,1,0:T(8,128)(2,1)}), bf16[16,72,768]{2,1,0:T(8,128)(2,1)}) %all-gather.11.cloned.1.call-update) | async-done | bytes 1769488 | tf_op jit(solution)/shard_map/all_gather | solution.py:411
  141.6 0.0 copy-done
  141.6 7.0 %convolution_convert_fusion.2 = bf16[1152,2048]{1,0:T(8,128)(2,1)} fusion(bf16[1152,768]{1,0:T(8,128)(2,1)} %bitcast.70, bf16[1,2048,768]{2,1,0:T(8,128)(2,1)S(1)} %copy-done), kind=kOutput, calls=%fused_computation.2 | convolution fusion | flops 3626237952 | bytes 9633792 | tf_op jit(solution)/shard_map/dot_general | solution.py:31
  148.7 0.0 reduce-scatter.2.cloned.1.call-update
  148.7 0.0 all-gather.9.cloned.1.call-start
  148.7 68.9 %all-gather.7.cloned.1.call-done = bf16[16,72,6144]{2,1,0:T(8,128)(2,1)} async-done(((bf16[16,72,768]{2,1,0:T(8,128)(2,1)}), bf16[16,72,6144]{2,1,0:T(8,128)(2,1)}) %all-gather.7.cloned.1.call-update) | async-done | bytes 14155792 | tf_op jit(solution)/shard_map/all_gather | solution.py:412
  217.7 8.7 %fusion.6 = f32[1152,256]{1,0:T(8,128)S(1)} fusion(bf16[1152,6144]{1,0:T(8,128)(2,1)} %bitcast.66, bf16[1,6144,256]{2,1,0:T(8,128)(2,1)} %param.17), kind=kOutput, calls=%fused_computation.11 | convolution fusion | flops 3623878656 | bytes 18481152 | tf_op jit(solution)/shard_map/dot_general | solution.py:31
  226.4 1.2 copy-done.11
  227.6 0.9 copy-done.12
  228.5 5.3 %multiply_convert_fusion = (bf16[1152,256]{1,0:T(8,128)(2,1)}, f32[1152,256]{1,0:T(8,128)}) fusion(f32[1152,256]{1,0:T(8,128)S(1)} %fusion.6, bf16[1152,6144]{1,0:T(8,128)(2,1)S(1)} %bitcast.69, bf16[1,6144,256]{2,1,0:T(8,128)(2,1)S(1)} %copy-done.12), kind=kOutput, calls=%fused_computation.25 | convolution fusion | flops 3625648128 | bytes 20250624 | tf_op jit(solution)/shard_map/dot_general | solution.py:31
  233.8 0.0 copy-done.14
  233.8 0.0 all-gather.9.cloned.1.call-update
  233.9 0.0 copy-done.4
  233.9 0.2 select_reduce_fusion.1
  234.1 0.5 slice_bitcast_fusion.1
  234.7 21.5 %reduce-scatter.2.cloned.1.call-done = bf16[1152,256]{1,0:T(8,128)(2,1)} async-done(((bf16[1152,2048]{1,0:T(8,128)(2,1)}), bf16[1152,256]{1,0:T(8,128)(2,1)}) %reduce-scatter.2.cloned.1.call-update) | async-done | bytes 589840 | tf_op jit(solution)/shard_map/reduce_scatter | solution.py:424
  256.2 12.1 %fusion = bf16[1,6144,256]{2,1,0:T(8,128)(2,1)} fusion(bf16[1152,6144]{1,0:T(8,128)(2,1)} %bitcast.67, f32[1152,256]{1,0:T(8,128)} %get-tuple-element.21, bf16[1152,256]{1,0:T(8,128)(2,1)} %reduce-scatter.2.cloned.1.call-done, f32[1152,256]{1,0:T(8,128)} %copy-done.14), kind=kOutput, calls=%fused_computation.3 | convolution fusion | flops 3628695552 | bytes 20250624 | tf_op jit(solution)/shard_map/dot_general | solution.py:31
  268.3 30.7 %all-gather.9.cloned.1.call-done = bf16[1152,2048]{1,0:T(8,128)(2,1)} async-done(((bf16[1152,256]{1,0:T(8,128)(2,1)}), bf16[1152,2048]{1,0:T(8,128)(2,1)}) %all-gather.9.cloned.1.call-update) | async-done | bytes 4718608 | tf_op jit(solution)/shard_map/all_gather | solution.py:418
  299.0 6.2 %convolution_convert_fusion.4 = bf16[1152,768]{1,0:T(8,128)(2,1)S(1)} fusion(bf16[1152,2048]{1,0:T(8,128)(2,1)} %all-gather.9.cloned.1.call-done, bf16[1,2048,768]{2,1,0:T(8,128)(2,1)S(1)} %copy-done), kind=kOutput, calls=%fused_computation.6 | convolution fusion | flops 3624763392 | bytes 9633792 | tf_op jit(solution)/shard_map/dot_general | solution.py:31
  305.2 1.4 copy.15
  306.5 6.7 %all-to-all-start = ((bf16[16,72,768]{2,1,0:T(8,128)(2,1)}), bf16[16,72,768]{2,1,0:T(8,128)(2,1)}, u32[]{:S(2)}, u32[]{:S(2)}) async-start(bf16[16,72,768]{2,1,0:T(8,128)(2,1)} %bitcast.62), calls=%async_computation | async-start | bytes 3538944 | tf_op jit(solution)/shard_map/all_to_all | solution.py:421
  313.3 11.9 %fusion.1 = bf16[1,6144,256]{2,1,0:T(8,128)(2,1)} fusion(bf16[1152,6144]{1,0:T(8,128)(2,1)} %bitcast.68, bf16[1152,256]{1,0:T(8,128)(2,1)} %reduce-scatter.2.cloned.1.call-done, f32[1152,256]{1,0:T(8,128)} %copy-done.14), kind=kOutput, calls=%fused_computation.4 | convolution fusion | flops 3627515904 | bytes 19070976 | tf_op jit(solution)/shard_map/dot_general | solution.py:31
  325.2 8.1 %fusion.8 = bf16[1,2048,768]{2,1,0:T(8,128)(2,1)} fusion(bf16[1152,2048]{1,0:T(8,128)(2,1)} %all-gather.9.cloned.1.call-done, bf16[1152,768]{1,0:T(8,128)(2,1)S(1)} %bitcast.71), kind=kOutput, calls=%fused_computation.13 | convolution fusion | flops 3625451520 | bytes 9633792 | tf_op jit(solution)/shard_map/dot_general | solution.py:31
  333.3 7.5 %all-to-all-done = bf16[16,72,768]{2,1,0:T(8,128)(2,1)} async-done(((bf16[16,72,768]{2,1,0:T(8,128)(2,1)}), bf16[16,72,768]{2,1,0:T(8,128)(2,1)}, u32[]{:S(2)}, u32[]{:S(2)}) %all-to-all-start) | async-done | bytes 1769504 | tf_op jit(solution)/shard_map/all_to_all | solution.py:421
  340.8 1.7 bitcast_reduce_fusion
  342.5 0.0 copy-done.10
  342.5 0.3 convolution_multiply_fusion
  342.8 1.1 fusion.10
  (17 shorter events, 0.0 us)
Async XLA Ops:
  7.2 134.5 %copy-start = (bf16[1,2048,768]{2,1,0:T(8,128)(2,1)S(1)}, bf16[1,2048,768]{2,1,0:T(8,128)(2,1)}, u32[]{:S(2)}) copy-start(bf16[1,2048,768]{2,1,0:T(8,128)(2,1)} %param.19) | copy-start | bytes 9437188
  7.2 104.1 %all-gather.5.cloned.1.call-start = ((), (), s32[]{:S(2)}) async-start(), calls=%async_computation.2 | async-start | bytes 2211840 | tf_op jit(solution)/shard_map/all_gather | solution.py:410
  8.1 0.7 copy-start.3
  8.8 1.1 copy-start.5
  9.9 0.9 copy-start.6
  10.8 0.9 copy-start.7
  11.7 0.9 copy-start.8
  12.7 0.7 copy-start.9
  85.0 0.8 copy-start.1
  85.7 0.8 copy-start.2
  86.5 55.1 %all-gather.11.cloned.1.call-start = ((), (), s32[]{:S(2)}) async-start(), calls=%async_computation.5 | async-start | bytes 2211840 | tf_op jit(solution)/shard_map/all_gather | solution.py:411
  87.3 130.4 %all-gather.7.cloned.1.call-start = ((), (), s32[]{:S(2)}) async-start(), calls=%async_computation.3 | async-start | bytes 15925248 | tf_op jit(solution)/shard_map/all_gather | solution.py:412
  111.3 144.9 %reduce-scatter.2.cloned.1.call-start = ((), (), s32[]{:S(2)}) async-start(), calls=%async_computation.6 | async-start | bytes 5308416 | tf_op jit(solution)/shard_map/reduce_scatter | solution.py:424
  148.7 150.3 %all-gather.9.cloned.1.call-start = ((), (), s32[]{:S(2)}) async-start(), calls=%async_computation.4 | async-start | bytes 5308416 | tf_op jit(solution)/shard_map/all_gather | solution.py:418
  217.7 9.9 %copy-start.11 = (bf16[16,72,6144]{2,1,0:T(8,128)(2,1)S(1)}, bf16[16,72,6144]{2,1,0:T(8,128)(2,1)}, u32[]{:S(2)}) copy-start(bf16[16,72,6144]{2,1,0:T(8,128)(2,1)} %all-gather.7.cloned.1.call-done) | copy-start | bytes 42467332
  217.7 10.8 %copy-start.12 = (bf16[1,6144,256]{2,1,0:T(8,128)(2,1)S(1)}, bf16[1,6144,256]{2,1,0:T(8,128)(2,1)}, u32[]{:S(2)}) copy-start(bf16[1,6144,256]{2,1,0:T(8,128)(2,1)} %param.18) | copy-start | bytes 9437188
  228.5 5.3 %copy-start.14 = (f32[1152,256]{1,0:T(8,128)}, f32[1152,256]{1,0:T(8,128)S(1)}, u32[]{:S(2)}) copy-start(f32[1152,256]{1,0:T(8,128)S(1)} %fusion.6) | copy-start | bytes 3538948
  228.5 5.4 %copy-start.4 = (s32[128,2]{0,1:T(2,128)S(1)}, s32[128,2]{0,1:T(2,128)}, u32[]{:S(2)}) copy-start(s32[128,2]{0,1:T(2,128)} %param.15) | copy-start | bytes 3076
  306.5 34.2 %all-to-all-start = ((bf16[16,72,768]{2,1,0:T(8,128)(2,1)}), bf16[16,72,768]{2,1,0:T(8,128)(2,1)}, u32[]{:S(2)}, u32[]{:S(2)}) async-start(bf16[16,72,768]{2,1,0:T(8,128)(2,1)} %bitcast.62), calls=%async_computation | async-start | bytes 3538944 | tf_op jit(solution)/shard_map/all_to_all | solution.py:421
  313.3 11.9 %copy-start.13 = (bf16[16,72,768]{2,1,0:T(8,128)(2,1)S(1)}, bf16[16,72,768]{2,1,0:T(8,128)(2,1)}, u32[]{:S(2)}) copy-start(bf16[16,72,768]{2,1,0:T(8,128)(2,1)} %all-gather.11.cloned.1.call-done) | copy-start | bytes 5308420
  333.3 9.2 %copy-start.10 = (f32[128]{0:T(128)S(1)}, f32[128]{0:T(128)}, u32[]{:S(2)}) copy-start(f32[128]{0:T(128)} %get-tuple-element.15) | copy-start | bytes 1540
Sparse Core Ops, SparseCore 0:
  86.6 24.5 all-gather.4
  113.5 28.0 all-gather.10
  143.3 74.2 all-gather.6
  219.9 36.2 reduce-scatter.1
  258.3 40.6 all-gather.8

commit v2 on v1

--- a/solution.py
+++ b/solution.py
@@ -161,10 +161,12 @@
     return jnp.sum(jnp.where(eye, row, 0.0), axis=1, keepdims=True)
 
 
-def front_kernel(
-    att, op, res, gain, rt, rts, cot,
-    state_o, xs_o, cs_o, pr_o,
+def layer_kernel(
+    att, op, res, gain, rt, rts, cot, gate_h, up_h, down_h,
+    out_h, gg_h, gu_h, gd_h,
+    state_o, pr_o,
     attb, own, sib16, sibr, r1, fin, st2, tot16, projr, stat, xrow, crow, xr, cr,
+    xb, wcat, wd, cb, acc, hid, sibd, sibdr, dst, dr1, dfin, dhf, dab, yst, yr1, yfin, zs, zr,
     ssem, rsem, lsem,
 ):
     x, y, z, c = coords()
@@ -182,6 +184,13 @@
         + group,
         turn,
     )
+    weights = [
+        pltpu.make_async_copy(gate_h, wcat.at[:, :, pl.ds(0, 256)], lsem.at[1]),
+        pltpu.make_async_copy(up_h, wcat.at[:, :, pl.ds(256, 256)], lsem.at[2]),
+        pltpu.make_async_copy(down_h, wd, lsem.at[3]),
+    ]
+    for copy in weights:
+        copy.start()
     attb[z, x] = att[...].reshape(attb.shape[2:])
 
     def quiet(ka, kb):
@@ -339,36 +348,256 @@
             jnp.where(m0, p0, 0.0) + jnp.where(m1, p1, 0.0), axis=1, keepdims=True
         )
         crow[e] = (crow[e].astype(F32) * share).astype(BF)
+    xr[z] = xrow[z]
+    cr[z] = crow[z]
+    for tag, ref in moved:
+        net.wait(tag, ref)
+
+    def pair(ref, f):
+        return jnp.concatenate(
+            [ref[2 * f].astype(F32), ref[2 * f + 1].astype(F32)], axis=0
+        ).astype(BF)
+
+    def along_x(k):
+        return dev(rot(x, k), y, z, c)
+
+    def along_y(k):
+        return dev(x, rot(y, k), z, c)
+
+    def sharing(at):
+        tags = {}
+
+        def share(ka, kb, at=at, tags=tags):
+            r = at(ka, kb, c)
+            tags[ka, kb] = net.send(r, r, mate)
+
+        def arrived(ka, kb, at=at, tags=tags):
+            net.wait(tags[ka, kb], at(ka, kb, 1 - c))
+
+        return share, arrived
+
+    for f in range(2):
+        xb[y, c, f, x] = pair(xr, f)
+    lo, hi = pl.ds(0, 80), pl.ds(80, 64)
+    share0, mate0 = sharing(lambda ka, kb, cc: xb.at[rot(y, kb), cc, 0, rot(x, ka)])
+    share1, mate1 = sharing(lambda ka, kb, cc: xb.at[rot(y, ka), cc, 1, rot(x, kb)])
+    g0 = Gather(net, lambda a, b: xb.at[b, c, 0, a], x, y, along_x, along_y, lo, hi, share0)
+    g1 = Gather(net, lambda a, b: xb.at[a, c, 1, b], y, x, along_y, along_x, lo, hi, share1)
+    flows = (g0, g1)
+    for g in flows:
+        g.begin()
+    moved = []
     for k in (1, 2, 3):
         e = rot(z, k)
         tag = net.send(crow.at[e], cr.at[z], dev(x, y, e, c))
         moved.append((tag, cr.at[rot(z, -k)]))
-    xr[z] = xrow[z]
-    cr[z] = crow[z]
+    for g in flows:
+        g.near_a()
+    for g in flows:
+        g.near_b(0)
+    for g in flows:
+        g.far_a()
     for tag, ref in moved:
         net.wait(tag, ref)
-    xs_o[...] = xr[...]
-    cs_o[...] = cr[...]
+    for f in range(2):
+        cb[f, x] = pair(cr, f)
+    gc = Gather(net, lambda a, b: cb.at[:, b], x, x, along_x, along_x, pl.ds(0, 1), pl.ds(1, 1), quiet)
+    for copy in weights:
+        copy.wait()
+
+    rows, hidden = xb.shape[4], hid.shape[-1]
+
+    def group0(kb, first):
+        for ka in (0, -1, 1, 2):
+            mate0(ka, kb)
+        yy = rot(y, kb)
+        for cc in range(2):
+            part = contract(
+                xb[yy, cc, 0].reshape(4 * rows, xb.shape[5]), wcat[2 * yy + cc], 1, 0
+            ).reshape(4, rows, 2 * hidden)
+            if first and cc == 0:
+                acc[0] = part
+            else:
+                acc[0] += part
+
+    def group1(kb):
+        for ka in (0, -1, 1, 2):
+            mate1(ka, kb)
+        xx = rot(x, kb)
+        total = jnp.zeros((rows, 2 * hidden), F32)
+        for h2 in range(8):
+            total += contract(xb[h2 // 2, h2 % 2, 1, xx], wcat[h2], 1, 0)
+        acc[1, xx] = total
+
+    for g in flows:
+        g.near_b(-1)
+    group0(0, True)
+    for g in flows:
+        g.near_b(1)
+    group1(0)
+    gc.along_b(0)
+    for k in (0, -1):
+        for g in flows:
+            g.far_b(k)
+    for g in flows:
+        g.near_b(2)
+    group1(-1)
+    group1(1)
+    group0(-1, False)
+    group0(1, False)
+    for k in (1, 2):
+        for g in flows:
+            g.far_b(k)
+    gc.near_b(0)
+
+    hshare, hmate = [], []
+    hg = []
+    for f in range(2):
+        s, m = sharing(lambda ka, kb, cc, f=f: hid.at[rot(y, kb), cc, f])
+        hmate.append(m)
+        hg.append(Gather(net, lambda a, b, f=f: hid.at[b, c, f], y, y, along_y, along_y, pl.ds(0, 2), pl.ds(2, 2), s))
+        hshare.append(s)
+
+    def activate(f):
+        a, b = acc[f, :, :, 0:hidden], acc[f, :, :, hidden : 2 * hidden]
+        hid[y, c, f] = (jax.nn.silu(a) * b).astype(BF)
+        hg[f].along_b(0)
+        hshare[f](0, 0)
+
+    group1(2)
+    activate(1)
+    group0(2, False)
+    activate(0)
+    gc.far_b(0)
+
+    def grad_hidden(yy, cc):
+        c_rows = cb[...].reshape(8 * rows, cb.shape[3])
+        return contract(c_rows, wd[2 * yy + cc], 1, 1).reshape(2, 4, rows, hidden)
+
+    tags = {}
+    for k in (2, -1, 1, 0):
+        yy = rot(y, k)
+        sibd[yy] = grad_hidden(yy, 1 - c).astype(BF)
+        tags[k] = net.send(sibd.at[yy], sibdr.at[yy], mate)
+    for f in (1, 0):
+        hg[f].near_b(0)
+    yy = rot(y, 2)
+    net.wait(tags[2], sibdr.at[yy])
+    dst[0] = (grad_hidden(yy, c) + sibdr[yy].astype(F32)).astype(BF)
+    ta = net.send(dst.at[0, 0], dr1.at[0], along_y(1))
+    tb = net.send(dst.at[0, 1], dr1.at[1], along_y(-1))
+    for f in (1, 0):
+        hg[f].far_b(0)
+    for f in (1, 0):
+        for kb in (0, -1, 1, 2):
+            hmate[f](0, kb)
+
+    def product_y(xx):
+        total = jnp.zeros((2 * rows, wd.shape[2]), F32)
+        for h2 in range(8):
+            part = hid[h2 // 2, h2 % 2, :, xx].reshape(2 * rows, hidden)
+            total += contract(part, wd[h2], 1, 0)
+        return total.reshape(2, rows, wd.shape[2])
+
+    yst[0] = product_y(rot(x, 2)).astype(BF)
+    tya = net.send(yst.at[0, 0], yr1.at[0], along_x(1))
+    tyb = net.send(yst.at[0, 1], yr1.at[1], along_x(-1))
+    for k, t, i in ((1, ta, 0), (-1, tb, 1)):
+        yy = rot(y, k)
+        net.wait(tags[k], sibdr.at[yy])
+        dhf[...] = grad_hidden(yy, c) + sibdr[yy].astype(F32)
+        net.wait(t, dr1.at[i])
+        dhf[i] += dr1[i].astype(F32)
+        dst[1 + i] = dhf[...].astype(BF)
+        tags["f", k] = net.send(dst.at[1 + i], dfin.at[i], along_y(k))
+    for k, t, i in ((1, tya, 0), (-1, tyb, 1)):
+        total = product_y(rot(x, k))
+        net.wait(t, yr1.at[i])
+        yst[1 + i, i] = (total[i] + yr1[i].astype(F32)).astype(BF)
+        yst[1 + i, 1 - i] = total[1 - i].astype(BF)
+        tags["y", k] = net.send(yst.at[1 + i], yfin.at[i], along_x(k))
+    total = product_y(x)
+    net.wait(tags[0], sibdr.at[y])
+    dhf[...] = grad_hidden(y, c) + sibdr[y].astype(F32)
+    net.wait(tags["y", 1], yfin.at[0])
+    net.wait(tags["y", -1], yfin.at[1])
+    total += yfin[0].astype(F32) + yfin[1].astype(F32)
+    for zz in range(4):
+        zs[zz] = total[zz // 2, (zz % 2) * zs.shape[1] : (zz % 2 + 1) * zs.shape[1]].astype(BF)
+    moved = []
+    for k in (1, 2, 3):
+        e = rot(z, k)
+        tag = net.send(zs.at[e], zr.at[z], dev(x, y, e, c))
+        moved.append((tag, zr.at[rot(z, -k)]))
+    zr[z] = zs[z]
+
+    writes = []
+
+    def write(src, dst_ref, sem):
+        copy = pltpu.make_async_copy(src, dst_ref, sem)
+        copy.start()
+        writes.append(copy)
+
+    for h2 in range(8):
+        part = hid[h2 // 2, h2 % 2].reshape(8 * rows, hidden)
+        wd[h2] = contract(part, cb[...].reshape(8 * rows, cb.shape[3]), 0, 0).astype(BF)
+        write(wd.at[h2], gd_h.at[h2], lsem.at[4 + h2])
+    for i, k in ((0, 1), (1, -1)):
+        net.wait(tags["f", k], dfin.at[i])
+    for f in range(2):
+        dh = dhf[f] + dfin[0, f].astype(F32) + dfin[1, f].astype(F32)
+        a, b = acc[f, :, :, 0:hidden], acc[f, :, :, hidden : 2 * hidden]
+        s = jax.nn.sigmoid(a)
+        dab[f, :, :, 0:hidden] = (dh * b * s * (1.0 + a * (1.0 - s))).astype(BF)
+        dab[f, :, :, hidden : 2 * hidden] = (dh * (a * s)).astype(BF)
+    for h2 in range(8):
+        part = xb[h2 // 2, h2 % 2].reshape(8 * rows, xb.shape[5])
+        wcat[h2] = contract(
+            part, dab[...].reshape(8 * rows, 2 * hidden), 0, 0
+        ).astype(BF)
+        write(wcat.at[h2, :, pl.ds(0, hidden)], gg_h.at[h2], lsem.at[12 + h2])
+        write(wcat.at[h2, :, pl.ds(hidden, hidden)], gu_h.at[h2], lsem.at[20 + h2])
+
+    for tag, ref in moved:
+        net.wait(tag, ref)
+    took0 = jnp.zeros(state_o.shape, F32)
+    took1 = jnp.zeros(state_o.shape, F32)
+    for e, (m0, m1) in enumerate(slot_masks(rts, capacity)):
+        took0 += contract(m0.astype(F32).astype(BF), zr[e], 0, 0)
+        took1 += contract(m1.astype(F32).astype(BF), zr[e], 0, 0)
+    out_h[...] = (
+        state_o[...] + as_column(pr_o[0:1, :]) * took0 + as_column(pr_o[1:2, :]) * took1
+    )
+    for copy in writes:
+        copy.wait()
     net.drain()
 
 
-def front(attention, out_proj, residual, norm_gain, router, routes, cotangent):
+def shards(
+    attention, out_proj, residual, norm_gain, router, routes, cotangent,
+    gate_weight, up_weight, down_weight,
+):
     vmem = pl.BlockSpec(memory_space=pltpu.VMEM)
+    hbm = pl.BlockSpec(memory_space=pl.ANY)
     rows, cols = attention.shape
     width = out_proj.shape[1]
     cap = rows * 9 // 16
+    pair_rows = 2 * cap
+    hidden = gate_weight.shape[2]
     sds = jax.ShapeDtypeStruct
-    return pl.pallas_call(
-        front_kernel,
+    layer_out, grad_gate, grad_up, grad_down = pl.pallas_call(
+        layer_kernel,
         out_shape=(
             sds((rows, cols), F32),
-            sds((4, cap, cols), BF),
-            sds((4, cap, cols), BF),
-            sds((8, rows), F32),
+            sds((8, cols, hidden), BF),
+            sds((8, cols, hidden), BF),
+            sds((8, hidden, cols), BF),
         ),
-        in_specs=[vmem] * 7,
-        out_specs=(vmem,) * 4,
+        in_specs=[vmem] * 7 + [hbm] * 3,
+        out_specs=(vmem,) + (hbm,) * 3,
         scratch_shapes=[
+            pltpu.VMEM((rows, cols), F32),
+            pltpu.VMEM((8, rows), F32),
             pltpu.VMEM((4, 4, 2, rows // 2, cols), BF),
             pltpu.VMEM((4, 2 * rows, width), F32),
             pltpu.VMEM((4, 2 * rows, width), BF),
@@ -383,15 +612,33 @@
             pltpu.VMEM((4, cap, cols), BF),
             pltpu.VMEM((4, cap, cols), BF),
             pltpu.VMEM((4, cap, cols), BF),
-            pltpu.SemaphoreType.DMA((64,)),
-            pltpu.SemaphoreType.DMA((64,)),
-            pltpu.SemaphoreType.DMA((1,)),
+            pltpu.VMEM((4, 2, 2, 4, pair_rows, cols), BF),
+            pltpu.VMEM((8, cols, 2 * hidden), BF),
+            pltpu.VMEM((8, hidden, cols), BF),
+            pltpu.VMEM((2, 4, pair_rows, cols), BF),
+            pltpu.VMEM((2, 4, pair_rows, 2 * hidden), F32),
+            pltpu.VMEM((4, 2, 2, 4, pair_rows, hidden), BF),
+            pltpu.VMEM((4, 2, 4, pair_rows, hidden), BF),
+            pltpu.VMEM((4, 2, 4, pair_rows, hidden), BF),
+            pltpu.VMEM((3, 2, 4, pair_rows, hidden), BF),
+            pltpu.VMEM((2, 4, pair_rows, hidden), BF),
+            pltpu.VMEM((2, 2, 4, pair_rows, hidden), BF),
+            pltpu.VMEM((2, 4, pair_rows, hidden), F32),
+            pltpu.VMEM((2, 4, pair_rows, 2 * hidden), BF),
+            pltpu.VMEM((3, 2, pair_rows, cols), BF),
+            pltpu.VMEM((2, pair_rows, cols), BF),
+            pltpu.VMEM((2, 2, pair_rows, cols), BF),
+            pltpu.VMEM((4, cap, cols), BF),
+            pltpu.VMEM((4, cap, cols), BF),
+            pltpu.SemaphoreType.DMA((208,)),
+            pltpu.SemaphoreType.DMA((208,)),
+            pltpu.SemaphoreType.DMA((28,)),
         ],
         compiler_params=pltpu.CompilerParams(
-            collective_id=0, has_side_effects=True, vmem_limit_bytes=40 * MIB
+            collective_id=0, has_side_effects=True, vmem_limit_bytes=63 * MIB
         ),
         cost_estimate=pl.CostEstimate(
-            flops=3_000_000_000, bytes_accessed=4_000_000, transcendentals=0
+            flops=30_000_000_000, bytes_accessed=25_000_000, transcendentals=0
         ),
     )(
         attention,
@@ -401,42 +648,16 @@
         router.T,
         routes.T,
         cotangent,
+        gate_weight.reshape(8, cols, hidden),
+        up_weight.reshape(8, cols, hidden),
+        down_weight.reshape(8, hidden, cols),
     )
-
-
-def shards(attention, out_proj, residual, norm_gain, router, routes, cotangent, gate_weight, up_weight, down_weight):
-    state, xs, cs, pr = front(attention, out_proj, residual, norm_gain, router, routes, cotangent)
-    groups = [[4 * z + x for x in range(4)] for z in range(4)]
-    xg = lax.all_gather(xs, "expert", axis=0, tiled=True, axis_index_groups=groups)
-    cg = lax.all_gather(cs, "expert", axis=0, tiled=True, axis_index_groups=groups)
-    x_rows = lax.all_gather(xg, "head", axis=2, tiled=True).reshape(1152, 6144)
-    cot_rows = cg.reshape(1152, 768)
-    gate_w = gate_weight[0]; up_w = up_weight[0]; down_w = down_weight[0]
-    g = contract(x_rows, gate_w, 1, 0); u = contract(x_rows, up_w, 1, 0)
-    act = jax.nn.silu(g)
-    hid = (act * u).astype(BF)
-    hid_all = lax.all_gather(hid, "head", axis=1, tiled=True)
-    yp = contract(hid_all, down_w, 1, 0).astype(BF)
-    yp = yp.reshape(4, 4, 72, 768).transpose(1, 0, 2, 3).reshape(16, 72, 768)
-    ret = lax.all_to_all(yp, "expert", split_axis=0, concat_axis=0, tiled=True).astype(F32)
-    slot_out = jnp.sum(ret.reshape(4, 4, 72, 768), axis=1).astype(BF).reshape(288, 768)
-    grad_down = contract(hid_all, cot_rows, 0, 0).astype(BF)
-    dh = lax.psum_scatter(contract(cot_rows, down_w, 1, 1).astype(BF), "head", scatter_dimension=1, tiled=True).astype(F32)
-    s = jax.nn.sigmoid(g)
-    da = (dh * u * s * (1.0 + g * (1.0 - s))).astype(BF)
-    db = (dh * act).astype(BF)
-    gg = contract(x_rows, da, 0, 0).astype(BF); gu = contract(x_rows, db, 0, 0).astype(BF)
-    r0, r1 = routes[:, 0], routes[:, 1]
-    ids = jnp.arange(4)
-    hits = ((r0[:, None] == ids) | (r1[:, None] == ids)).astype(F32)
-    earlier = jnp.dot(jnp.tril(jnp.ones((128, 128), F32), -1), hits)
-    s0 = jnp.sum(jnp.where(r0[:, None] == ids, earlier, 0), axis=1).astype(jnp.int32) + r0 * 72
-    s1 = jnp.sum(jnp.where(r1[:, None] == ids, earlier, 0), axis=1).astype(jnp.int32) + r1 * 72
-    rid = jnp.arange(288)
-    t0 = jnp.dot((s0[:, None] == rid).astype(BF), slot_out, preferred_element_type=F32)
-    t1 = jnp.dot((s1[:, None] == rid).astype(BF), slot_out, preferred_element_type=F32)
-    out = state + pr[0][:, None] * t0 + pr[1][:, None] * t1
-    return out, gg[None], gu[None], grad_down[None]
+    return (
+        layer_out,
+        grad_gate.reshape(gate_weight.shape),
+        grad_up.reshape(up_weight.shape),
+        grad_down.reshape(down_weight.shape),
+    )
 
 
 def solution(mesh):

time: 351 us -> 193 us (0.55)
  waiting for transfers between devices: 184 us -> 0 us
  Pallas kernels: 71.6 us -> 180 us
  matrix products: 61 us -> 0 us
  between operations: 13.9 us -> 0.64 us
  starting transfers between devices: 6.92 us -> 0 us
    all_gather x4 -> x0, waiting for transfers between devices: 154 us -> none  [the longest x1 68.9 us: shards(): x_rows = lax.all_gather(xg, 'head', axis=2, tiled=True).reshape(1152, 6144)]
    pallas_call x1, Pallas kernels: 71.6 us -> 180 us  [shards(): pl.pallas_call(layer_kernel, out_shape=(sds((rows, cols), F32), sds((8, c...]
    dot_general x10 -> x0, matrix products: 61 us -> none  [the longest x7 59.4 us: contract(): lax.dot_general(a, b, (((ca,), (cb,)), ((), ())), preferred_element_type=...]
    reduce_scatter x1 -> x0, waiting for transfers between devices: 21.5 us -> none  [shards(): lax.psum_scatter(contract(cot_rows, down_w, 1, 1).astype(BF), 'head', sca...]
    all_to_all x1 -> x0, waiting for transfers between devices: 7.49 us -> none  [shards(): lax.all_to_all(yp, 'expert', split_axis=0, concat_axis=0, tiled=True)]
    all_to_all x1 -> x0, starting transfers between devices: 6.72 us -> none  [shards(): lax.all_to_all(yp, 'expert', split_axis=0, concat_axis=0, tiled=True)]
    unnamed x30 -> x8, local copies, waits for them, and re-layouts: 8.92 us -> 10.4 us
  transfers between devices with their start and end apart: 6 -> 0, of which waited for: 6 -> 0; matrix products, arithmetic and copies ran while one was open for 15% -> 0% of each run, Pallas kernels for 0% -> 0%
where the time goes in v2:
time: 193 us
  Pallas kernels  180 us (93%)
  local copies, waits for them, and re-layouts  11.6 us (6%)
    pallas_call x1, Pallas kernels, shards(): pl.pallas_call(layer_kernel, out_shape=(sds((rows, cols), F32), sds((8, c...  180 us
    unnamed x8, local copies, waits for them, and re-layouts  10.4 us

profile of v2, /device:TPU:1, one launch (start us, length us, event | category | flops | bytes accessed | tf_op | source)
XLA Modules:
  0.0 192.7 jit_solution(5785171344293603308)
XLA Ops:
  0.6 1.3 broadcast_in_dim.3.gain
  1.9 180.5 %shard_map.129 = (f32[128,768]{1,0:T(8,128)}, bf16[8,768,256]{2,1,0:T(8,128)(2,1)}, bf16[8,768,256]{2,1,0:T(8,128)(2,1)}, bf16[8,256,768]{2,1,0:T(8,128)(2,1)}) custom-call(bf16[128,768]{1,0:T(8,128)(2,1)} %att.1, bf16[768,384]{1,0:T(8,128)(2,1)} %op.1, bf16[128,768]{1,0:T(8,128)(2,1)} %res.1, bf16[1,768]{1,0:T(2,128)(2,1)} %broadcast_in_dim.3.gain, ...), custom_call_target="tpu_custom_call" | custom-call | flops 30000001024 | bytes 25000000 | tf_op jit(solution)/shard_map/pallas_call | solution.py:588
  182.4 1.8 copy.18
  184.1 0.0 copy-start.1
  184.1 3.9 %copy.19 = bf16[1,6144,256]{2,1,0:T(8,128)(2,1)} copy(bf16[1,6144,256]{2,1,0:T(8,128)(2,1)} %bitcast.10) | data formatting | bytes 6291456
  188.0 0.0 copy-done.1
  188.0 0.0 copy-start
  188.1 1.7 copy.20
  189.7 1.4 copy-done
  191.1 1.7 copy.21
Async XLA Ops:
  184.1 3.9 %copy-start.1 = (bf16[8,768,256]{2,1,0:T(8,128)(2,1)S(1)}, bf16[8,768,256]{2,1,0:T(8,128)(2,1)}, u32[]{:S(2)}) copy-start(bf16[8,768,256]{2,1,0:T(8,128)(2,1)} %get-tuple-element.10) | copy-start | bytes 9437188
  188.0 3.0 %copy-start = (bf16[8,256,768]{2,1,0:T(8,128)(2,1)S(1)}, bf16[8,256,768]{2,1,0:T(8,128)(2,1)}, u32[]{:S(2)}) copy-start(bf16[8,256,768]{2,1,0:T(8,128)(2,1)} %get-tuple-element.11) | copy-start | bytes 9437188

commit v3 on v2

--- a/solution.py
+++ b/solution.py
@@ -36,7 +36,7 @@
 class Net:
     def __init__(self, ssem, rsem, mate):
         self.ssem, self.rsem, self.mate = ssem, rsem, mate
-        self.n, self.sent = 0, []
+        self.n, self.sent = 0, {}
 
     def send(self, src, dst, to):
         tag = self.n
@@ -50,7 +50,7 @@
             device_id_type=MESH,
         )
         copy.start()
-        self.sent.append(copy)
+        self.sent[tag] = copy
         return tag
 
     def wait(self, tag, dst):
@@ -64,9 +64,11 @@
         ).wait_recv()
 
     def drain(self):
-        for copy in self.sent:
-            copy.wait_send()
-        self.sent = []
+        for tag in list(self.sent):
+            self.left(tag)
+
+    def left(self, tag):
+        self.sent.pop(tag).wait_send()
 
 
 class Gather:
@@ -166,7 +168,7 @@
     out_h, gg_h, gu_h, gd_h,
     state_o, pr_o,
     attb, own, sib16, sibr, r1, fin, st2, tot16, projr, stat, xrow, crow, xr, cr,
-    xb, wcat, wd, cb, acc, hid, sibd, sibdr, dst, dr1, dfin, dhf, dab, yst, yr1, yfin, zs, zr,
+    xb, wcat, wd, cb, acc, hid, sibd, sibdr, dst, dr1, dfin, dhf, dab, pcol, prow, pz, pall, yst, yr1, yfin, ysum, yvia, zs, zr,
     ssem, rsem, lsem,
 ):
     x, y, z, c = coords()
@@ -179,7 +181,7 @@
         for k in range(1, 8)
     ]
     greet(
-        [dev(rot(x, 1), y, z, c), dev(rot(x, -1), y, z, c)]
+        [dev(rot(x, k), y, z, c) for k in (1, 2, 3)]
         + [dev(x, y, rot(z, k), c) for k in (1, 2, 3)]
         + group,
         turn,
@@ -196,6 +198,17 @@
     def quiet(ka, kb):
         pass
 
+    def pair(ref, f):
+        return jnp.concatenate(
+            [ref[2 * f].astype(F32), ref[2 * f + 1].astype(F32)], axis=0
+        ).astype(BF)
+
+    def along_x(k):
+        return dev(rot(x, k), y, z, c)
+
+    def along_y(k):
+        return dev(x, rot(y, k), z, c)
+
     lo, hi = pl.ds(0, 32), pl.ds(32, 32)
     g0 = Gather(net, lambda a, b: attb.at[b, a, 0], x, z, lambda k: dev(rot(x, k), y, z, c), lambda k: dev(x, y, rot(z, k), c), lo, hi, quiet)
     g1 = Gather(net, lambda a, b: attb.at[a, b, 1], z, x, lambda k: dev(x, y, rot(z, k), c), lambda k: dev(rot(x, k), y, z, c), lo, hi, quiet)
@@ -207,6 +220,7 @@
     for e, (m0, m1) in enumerate(masks):
         pick = (m0 | m1).astype(F32).astype(BF)
         crow[e] = contract(pick, cot[...], 1, 0).astype(BF)
+    cr[z] = crow[z]
     for g in flows:
         g.near_a()
     for g in flows:
@@ -221,6 +235,11 @@
             g.far_b(k)
     for g in flows:
         g.near_b(2)
+    cmoved = []
+    for k in (1, 2, 3):
+        e = rot(z, k)
+        tag = net.send(crow.at[e], cr.at[z], dev(x, y, e, c))
+        cmoved.append((tag, cr.at[rot(z, -k)]))
     for k in (1, 2):
         for g in flows:
             g.far_b(k)
@@ -247,6 +266,12 @@
             tb = net.send(
                 st2.at[0, pl.ds(128, 128)], r1.at[1], dev(x, rot(y, -1), z, c)
             )
+    for tag, ref in cmoved:
+        net.wait(tag, ref)
+    for f in range(2):
+        cb[f, x] = pair(cr, f)
+    gc = Gather(net, lambda a, b: cb.at[:, b], x, x, along_x, along_x, pl.ds(0, 1), pl.ds(1, 1), quiet)
+    gc.along_b(0)
     net.wait(ta, r1.at[0])
     yy = rot(y, 1)
     own[yy, 0:128, :] += r1[0].astype(F32)
@@ -285,6 +310,7 @@
         def _(remote=remote):
             remote().start()
 
+    gc.near_b(0)
     for k in range(2):
         local = (x == 2 * c + k) & (y == z) & (c == x // 2)
 
@@ -320,6 +346,21 @@
     squares = contract(ones, state * state, 1, 1, precision=lax.Precision.HIGHEST)
     stat[h, 4:8, :] = squares[0:4]
     tags = [net.send(stat.at[h], stat.at[h], d) for d in group]
+    rows, hidden = xb.shape[4], hid.shape[-1]
+    for copy in weights:
+        copy.wait()
+    gc.far_b(0)
+
+    def grad_hidden(yy, cc):
+        c_rows = cb[...].reshape(8 * rows, cb.shape[3])
+        return contract(c_rows, wd[2 * yy + cc], 1, 1).reshape(2, 4, rows, hidden)
+
+    dtags = {}
+    for k in (2, -1, 1, 0):
+        yy = rot(y, k)
+        sibd[yy] = grad_hidden(yy, 1 - c).astype(BF)
+        dtags[k] = net.send(sibd.at[yy], sibdr.at[yy], mate)
+
     for k, tag in enumerate(tags):
         net.wait(tag, stat.at[lax.rem(h + 7 - k, 8)])
     sums = stat[0]
@@ -343,26 +384,26 @@
         e = rot(z, k)
         tag = net.send(xrow.at[e], xr.at[z], dev(x, y, e, c))
         moved.append((tag, xr.at[rot(z, -k)]))
+    xr[z] = xrow[z]
+    both = jnp.concatenate([p0, p1, jnp.zeros((6, p0.shape[1]), F32)], axis=0)
     for e, (m0, m1) in enumerate(masks):
-        share = jnp.sum(
-            jnp.where(m0, p0, 0.0) + jnp.where(m1, p1, 0.0), axis=1, keepdims=True
-        )
-        crow[e] = (crow[e].astype(F32) * share).astype(BF)
-    xr[z] = xrow[z]
-    cr[z] = crow[z]
+        first = contract(both, m0.astype(F32), 1, 1, precision=lax.Precision.HIGHEST)
+        second = contract(both, m1.astype(F32), 1, 1, precision=lax.Precision.HIGHEST)
+        prow[e] = jnp.zeros(prow.shape[1:], F32)
+        prow[e, 0:1, 0:capacity] = first[0:1] + second[1:2]
+    pmoved = []
+    for k in (1, 2, 3):
+        e = rot(z, k)
+        tag = net.send(prow.at[e], pz.at[z], dev(x, y, e, c))
+        pmoved.append((tag, pz.at[rot(z, -k)]))
+    pz[z] = prow[z]
+    yy = rot(y, 2)
+    net.wait(dtags[2], sibdr.at[yy])
+    dst[0] = (grad_hidden(yy, c) + sibdr[yy].astype(F32)).astype(BF)
+    dta = net.send(dst.at[0, 0], dr1.at[0], along_y(1))
+    dtb = net.send(dst.at[0, 1], dr1.at[1], along_y(-1))
     for tag, ref in moved:
         net.wait(tag, ref)
-
-    def pair(ref, f):
-        return jnp.concatenate(
-            [ref[2 * f].astype(F32), ref[2 * f + 1].astype(F32)], axis=0
-        ).astype(BF)
-
-    def along_x(k):
-        return dev(rot(x, k), y, z, c)
-
-    def along_y(k):
-        return dev(x, rot(y, k), z, c)
 
     def sharing(at):
         tags = {}
@@ -386,26 +427,19 @@
     flows = (g0, g1)
     for g in flows:
         g.begin()
-    moved = []
+    for g in flows:
+        g.near_a()
+    for g in flows:
+        g.near_b(0)
+    for g in flows:
+        g.far_a()
+    for tag, ref in pmoved:
+        net.wait(tag, ref)
+    pall[x] = pz[...]
+    ptags = []
     for k in (1, 2, 3):
-        e = rot(z, k)
-        tag = net.send(crow.at[e], cr.at[z], dev(x, y, e, c))
-        moved.append((tag, cr.at[rot(z, -k)]))
-    for g in flows:
-        g.near_a()
-    for g in flows:
-        g.near_b(0)
-    for g in flows:
-        g.far_a()
-    for tag, ref in moved:
-        net.wait(tag, ref)
-    for f in range(2):
-        cb[f, x] = pair(cr, f)
-    gc = Gather(net, lambda a, b: cb.at[:, b], x, x, along_x, along_x, pl.ds(0, 1), pl.ds(1, 1), quiet)
-    for copy in weights:
-        copy.wait()
-
-    rows, hidden = xb.shape[4], hid.shape[-1]
+        tag = net.send(pall.at[x], pall.at[x], along_x(k))
+        ptags.append((tag, pall.at[rot(x, -k)]))
 
     def group0(kb, first):
         for ka in (0, -1, 1, 2):
@@ -435,12 +469,19 @@
     for g in flows:
         g.near_b(1)
     group1(0)
-    gc.along_b(0)
     for k in (0, -1):
         for g in flows:
             g.far_b(k)
     for g in flows:
         g.near_b(2)
+    for k, t, i in ((1, dta, 0), (-1, dtb, 1)):
+        yy = rot(y, k)
+        net.wait(dtags[k], sibdr.at[yy])
+        dhf[...] = grad_hidden(yy, c) + sibdr[yy].astype(F32)
+        net.wait(t, dr1.at[i])
+        dhf[i] += dr1[i].astype(F32)
+        dst[1 + i] = dhf[...].astype(BF)
+        dtags["f", k] = net.send(dst.at[1 + i], dfin.at[i], along_y(k))
     group1(-1)
     group1(1)
     group0(-1, False)
@@ -448,7 +489,6 @@
     for k in (1, 2):
         for g in flows:
             g.far_b(k)
-    gc.near_b(0)
 
     hshare, hmate = [], []
     hg = []
@@ -468,68 +508,17 @@
     activate(1)
     group0(2, False)
     activate(0)
-    gc.far_b(0)
-
-    def grad_hidden(yy, cc):
-        c_rows = cb[...].reshape(8 * rows, cb.shape[3])
-        return contract(c_rows, wd[2 * yy + cc], 1, 1).reshape(2, 4, rows, hidden)
-
-    tags = {}
-    for k in (2, -1, 1, 0):
-        yy = rot(y, k)
-        sibd[yy] = grad_hidden(yy, 1 - c).astype(BF)
-        tags[k] = net.send(sibd.at[yy], sibdr.at[yy], mate)
-    for f in (1, 0):
-        hg[f].near_b(0)
-    yy = rot(y, 2)
-    net.wait(tags[2], sibdr.at[yy])
-    dst[0] = (grad_hidden(yy, c) + sibdr[yy].astype(F32)).astype(BF)
-    ta = net.send(dst.at[0, 0], dr1.at[0], along_y(1))
-    tb = net.send(dst.at[0, 1], dr1.at[1], along_y(-1))
-    for f in (1, 0):
-        hg[f].far_b(0)
-    for f in (1, 0):
-        for kb in (0, -1, 1, 2):
-            hmate[f](0, kb)
-
-    def product_y(xx):
-        total = jnp.zeros((2 * rows, wd.shape[2]), F32)
-        for h2 in range(8):
-            part = hid[h2 // 2, h2 % 2, :, xx].reshape(2 * rows, hidden)
-            total += contract(part, wd[h2], 1, 0)
-        return total.reshape(2, rows, wd.shape[2])
-
-    yst[0] = product_y(rot(x, 2)).astype(BF)
-    tya = net.send(yst.at[0, 0], yr1.at[0], along_x(1))
-    tyb = net.send(yst.at[0, 1], yr1.at[1], along_x(-1))
-    for k, t, i in ((1, ta, 0), (-1, tb, 1)):
-        yy = rot(y, k)
-        net.wait(tags[k], sibdr.at[yy])
-        dhf[...] = grad_hidden(yy, c) + sibdr[yy].astype(F32)
-        net.wait(t, dr1.at[i])
-        dhf[i] += dr1[i].astype(F32)
-        dst[1 + i] = dhf[...].astype(BF)
-        tags["f", k] = net.send(dst.at[1 + i], dfin.at[i], along_y(k))
-    for k, t, i in ((1, tya, 0), (-1, tyb, 1)):
-        total = product_y(rot(x, k))
-        net.wait(t, yr1.at[i])
-        yst[1 + i, i] = (total[i] + yr1[i].astype(F32)).astype(BF)
-        yst[1 + i, 1 - i] = total[1 - i].astype(BF)
-        tags["y", k] = net.send(yst.at[1 + i], yfin.at[i], along_x(k))
-    total = product_y(x)
-    net.wait(tags[0], sibdr.at[y])
+    net.wait(dtags[0], sibdr.at[y])
     dhf[...] = grad_hidden(y, c) + sibdr[y].astype(F32)
-    net.wait(tags["y", 1], yfin.at[0])
-    net.wait(tags["y", -1], yfin.at[1])
-    total += yfin[0].astype(F32) + yfin[1].astype(F32)
-    for zz in range(4):
-        zs[zz] = total[zz // 2, (zz % 2) * zs.shape[1] : (zz % 2 + 1) * zs.shape[1]].astype(BF)
-    moved = []
-    for k in (1, 2, 3):
-        e = rot(z, k)
-        tag = net.send(zs.at[e], zr.at[z], dev(x, y, e, c))
-        moved.append((tag, zr.at[rot(z, -k)]))
-    zr[z] = zs[z]
+    for tag, ref in ptags:
+        net.wait(tag, ref)
+    for tag in gc.t.values():
+        net.left(tag)
+    for f in range(2):
+        for xx in range(4):
+            cols = [as_column(pall[xx, 2 * f + i, 0:1, :])[0:capacity] for i in range(2)]
+            pcol[f, xx] = jnp.concatenate(cols, axis=0)
+            cb[f, xx] = (cb[f, xx].astype(F32) * pcol[f, xx]).astype(BF)
 
     writes = []
 
@@ -538,19 +527,7 @@
         copy.start()
         writes.append(copy)
 
-    for h2 in range(8):
-        part = hid[h2 // 2, h2 % 2].reshape(8 * rows, hidden)
-        wd[h2] = contract(part, cb[...].reshape(8 * rows, cb.shape[3]), 0, 0).astype(BF)
-        write(wd.at[h2], gd_h.at[h2], lsem.at[4 + h2])
-    for i, k in ((0, 1), (1, -1)):
-        net.wait(tags["f", k], dfin.at[i])
-    for f in range(2):
-        dh = dhf[f] + dfin[0, f].astype(F32) + dfin[1, f].astype(F32)
-        a, b = acc[f, :, :, 0:hidden], acc[f, :, :, hidden : 2 * hidden]
-        s = jax.nn.sigmoid(a)
-        dab[f, :, :, 0:hidden] = (dh * b * s * (1.0 + a * (1.0 - s))).astype(BF)
-        dab[f, :, :, hidden : 2 * hidden] = (dh * (a * s)).astype(BF)
-    for h2 in range(8):
+    def grads(h2):
         part = xb[h2 // 2, h2 % 2].reshape(8 * rows, xb.shape[5])
         wcat[h2] = contract(
             part, dab[...].reshape(8 * rows, 2 * hidden), 0, 0
@@ -558,8 +535,99 @@
         write(wcat.at[h2, :, pl.ds(0, hidden)], gg_h.at[h2], lsem.at[12 + h2])
         write(wcat.at[h2, :, pl.ds(hidden, hidden)], gu_h.at[h2], lsem.at[20 + h2])
 
-    for tag, ref in moved:
-        net.wait(tag, ref)
+    def grads_down(h2):
+        part = hid[h2 // 2, h2 % 2].reshape(8 * rows, hidden)
+        wd[h2] = contract(part, cb[...].reshape(8 * rows, cb.shape[3]), 0, 0).astype(BF)
+        write(wd.at[h2], gd_h.at[h2], lsem.at[4 + h2])
+
+    for i, k in ((0, 1), (1, -1)):
+        net.wait(dtags["f", k], dfin.at[i])
+    for f in range(2):
+        dh = dhf[f] + dfin[0, f].astype(F32) + dfin[1, f].astype(F32)
+        dh = dh * pcol[f]
+        a, b = acc[f, :, :, 0:hidden], acc[f, :, :, hidden : 2 * hidden]
+        s = jax.nn.sigmoid(a)
+        dab[f, :, :, 0:hidden] = (dh * b * s * (1.0 + a * (1.0 - s))).astype(BF)
+        dab[f, :, :, hidden : 2 * hidden] = (dh * (a * s)).astype(BF)
+    def product_y(f, xx):
+        total = jnp.zeros((rows, wd.shape[2]), F32)
+        for h2 in range(8):
+            total += contract(hid[h2 // 2, h2 % 2, f, xx], wd[h2], 1, 0)
+        return total
+
+    ytags = {}
+
+    def expert_rows(f, block):
+        via = 1 if f == 0 else -1
+        yst[0, f] = product_y(f, rot(x, 2)).astype(BF)
+        first = net.send(yst.at[0, f], yr1.at[f], along_x(via))
+        yst[1, f] = product_y(f, rot(x, -via)).astype(BF)
+        ytags[f, -via] = net.send(yst.at[1, f], yfin.at[1, f], along_x(-via))
+        yvia[...] = product_y(f, rot(x, via))
+        ysum[f] = product_y(f, x)
+        grads(block)
+        net.wait(first, yr1.at[f])
+        yst[2, f] = (yvia[...] + yr1[f].astype(F32)).astype(BF)
+        ytags[f, via] = net.send(yst.at[2, f], yfin.at[0, f], along_x(via))
+
+    zbase = net.n
+    net.n += 4
+
+    def to_plane(zz):
+        return pltpu.make_async_remote_copy(
+            src_ref=zs.at[zz],
+            dst_ref=zr.at[z],
+            send_sem=ssem.at[zbase + zz],
+            recv_sem=rsem.at[zbase + z],
+            device_id=dev(x, y, zz, c),
+            device_id_type=MESH,
+        )
+
+    def to_owners(f):
+        via = 1 if f == 0 else -1
+        net.wait(ytags[f, -via], yfin.at[1, f])
+        net.wait(ytags[f, via], yfin.at[0, f])
+        total = ysum[f] + yfin[0, f].astype(F32) + yfin[1, f].astype(F32)
+        for i in range(2):
+            zz = 2 * f + i
+            zs[zz] = total[i * capacity : (i + 1) * capacity].astype(BF)
+
+            @pl.when(z != zz)
+            def _(zz=zz):
+                to_plane(zz).start()
+
+    def arrive(f):
+        hg[f].far_b(0)
+        for kb in (0, -1, 1, 2):
+            hmate[f](0, kb)
+
+    hg[1].near_b(0)
+    grads(0)
+    hg[0].near_b(0)
+    for h2 in (1, 2, 3):
+        grads(h2)
+    arrive(1)
+    expert_rows(1, 4)
+    grads(5)
+    arrive(0)
+    expert_rows(0, 6)
+    to_owners(1)
+    for h2 in range(6):
+        grads_down(h2)
+    to_owners(0)
+    for h2 in (6, 7):
+        grads_down(h2)
+    grads(7)
+    zr[z] = zs[z]
+    for k in (1, 2, 3):
+        zz = rot(z, k)
+        net.wait(zbase + zz, zr.at[zz])
+    for zz in range(4):
+
+        @pl.when(z != zz)
+        def _(zz=zz):
+            to_plane(zz).wait_send()
+
     took0 = jnp.zeros(state_o.shape, F32)
     took1 = jnp.zeros(state_o.shape, F32)
     for e, (m0, m1) in enumerate(slot_masks(rts, capacity)):
@@ -625,13 +693,19 @@
             pltpu.VMEM((2, 2, 4, pair_rows, hidden), BF),
             pltpu.VMEM((2, 4, pair_rows, hidden), F32),
             pltpu.VMEM((2, 4, pair_rows, 2 * hidden), BF),
+            pltpu.VMEM((2, 4, pair_rows, 1), F32),
+            pltpu.VMEM((4, 8, rows), F32),
+            pltpu.VMEM((4, 8, rows), F32),
+            pltpu.VMEM((4, 4, 8, rows), F32),
             pltpu.VMEM((3, 2, pair_rows, cols), BF),
             pltpu.VMEM((2, pair_rows, cols), BF),
             pltpu.VMEM((2, 2, pair_rows, cols), BF),
+            pltpu.VMEM((2, pair_rows, cols), F32),
+            pltpu.VMEM((pair_rows, cols), F32),
             pltpu.VMEM((4, cap, cols), BF),
             pltpu.VMEM((4, cap, cols), BF),
-            pltpu.SemaphoreType.DMA((208,)),
-            pltpu.SemaphoreType.DMA((208,)),
+            pltpu.SemaphoreType.DMA((216,)),
+            pltpu.SemaphoreType.DMA((216,)),
             pltpu.SemaphoreType.DMA((28,)),
         ],
         compiler_params=pltpu.CompilerParams(

time: 193 us -> 188 us (0.974)
  Pallas kernels: 180 us -> 176 us
    pallas_call x1, Pallas kernels: 180 us -> 176 us  [shards(): pl.pallas_call(layer_kernel, out_shape=(sds((rows, cols), F32), sds((8, c...]
where the time goes in v3:
time: 188 us
  Pallas kernels  176 us (94%)
  local copies, waits for them, and re-layouts  11.6 us (6%)
    pallas_call x1, Pallas kernels, shards(): pl.pallas_call(layer_kernel, out_shape=(sds((rows, cols), F32), sds((8, c...  176 us
    unnamed x8, local copies, waits for them, and re-layouts  10.4 us

profile of v3, /device:TPU:1, one launch (start us, length us, event | category | flops | bytes accessed | tf_op | source)
XLA Modules:
  0.0 187.9 jit_solution(5452449903965862841)
XLA Ops:
  0.6 1.3 broadcast_in_dim.3.gain
  1.9 175.6 %shard_map.129 = (f32[128,768]{1,0:T(8,128)}, bf16[8,768,256]{2,1,0:T(8,128)(2,1)}, bf16[8,768,256]{2,1,0:T(8,128)(2,1)}, bf16[8,256,768]{2,1,0:T(8,128)(2,1)}) custom-call(bf16[128,768]{1,0:T(8,128)(2,1)} %att.1, bf16[768,384]{1,0:T(8,128)(2,1)} %op.1, bf16[128,768]{1,0:T(8,128)(2,1)} %res.1, bf16[1,768]{1,0:T(2,128)(2,1)} %broadcast_in_dim.3.gain, ...), custom_call_target="tpu_custom_call" | custom-call | flops 30000001024 | bytes 25000000 | tf_op jit(solution)/shard_map/pallas_call | solution.py:656
  177.5 1.8 copy.18
  179.3 0.0 copy-start.1
  179.3 3.9 %copy.19 = bf16[1,6144,256]{2,1,0:T(8,128)(2,1)} copy(bf16[1,6144,256]{2,1,0:T(8,128)(2,1)} %bitcast.10) | data formatting | bytes 6291456
  183.2 0.0 copy-done.1
  183.2 0.0 copy-start
  183.2 1.7 copy.20
  184.9 1.4 copy-done
  186.2 1.7 copy.21
Async XLA Ops:
  179.3 3.9 %copy-start.1 = (bf16[8,768,256]{2,1,0:T(8,128)(2,1)S(1)}, bf16[8,768,256]{2,1,0:T(8,128)(2,1)}, u32[]{:S(2)}) copy-start(bf16[8,768,256]{2,1,0:T(8,128)(2,1)} %get-tuple-element.10) | copy-start | bytes 9437188
  183.2 3.0 %copy-start = (bf16[8,256,768]{2,1,0:T(8,128)(2,1)S(1)}, bf16[8,256,768]{2,1,0:T(8,128)(2,1)}, u32[]{:S(2)}) copy-start(bf16[8,256,768]{2,1,0:T(8,128)(2,1)} %get-tuple-element.11) | copy-start | bytes 9437188

commit v4 on v3

--- a/solution.py
+++ b/solution.py
@@ -346,21 +346,6 @@
     squares = contract(ones, state * state, 1, 1, precision=lax.Precision.HIGHEST)
     stat[h, 4:8, :] = squares[0:4]
     tags = [net.send(stat.at[h], stat.at[h], d) for d in group]
-    rows, hidden = xb.shape[4], hid.shape[-1]
-    for copy in weights:
-        copy.wait()
-    gc.far_b(0)
-
-    def grad_hidden(yy, cc):
-        c_rows = cb[...].reshape(8 * rows, cb.shape[3])
-        return contract(c_rows, wd[2 * yy + cc], 1, 1).reshape(2, 4, rows, hidden)
-
-    dtags = {}
-    for k in (2, -1, 1, 0):
-        yy = rot(y, k)
-        sibd[yy] = grad_hidden(yy, 1 - c).astype(BF)
-        dtags[k] = net.send(sibd.at[yy], sibdr.at[yy], mate)
-
     for k, tag in enumerate(tags):
         net.wait(tag, stat.at[lax.rem(h + 7 - k, 8)])
     sums = stat[0]
@@ -397,6 +382,21 @@
         tag = net.send(prow.at[e], pz.at[z], dev(x, y, e, c))
         pmoved.append((tag, pz.at[rot(z, -k)]))
     pz[z] = prow[z]
+    rows, hidden = xb.shape[4], hid.shape[-1]
+    for copy in weights:
+        copy.wait()
+    gc.far_b(0)
+
+    def grad_hidden(yy, cc):
+        c_rows = cb[...].reshape(8 * rows, cb.shape[3])
+        return contract(c_rows, wd[2 * yy + cc], 1, 1).reshape(2, 4, rows, hidden)
+
+    dtags = {}
+    for k in (2, -1, 1, 0):
+        yy = rot(y, k)
+        sibd[yy] = grad_hidden(yy, 1 - c).astype(BF)
+        dtags[k] = net.send(sibd.at[yy], sibdr.at[yy], mate)
+
     yy = rot(y, 2)
     net.wait(dtags[2], sibdr.at[yy])
     dst[0] = (grad_hidden(yy, c) + sibdr[yy].astype(F32)).astype(BF)

time: 188 us -> 191 us (1.016)
  Pallas kernels: 176 us -> 179 us
    pallas_call x1, Pallas kernels: 176 us -> 179 us  [shards(): pl.pallas_call(layer_kernel, out_shape=(sds((rows, cols), F32), sds((8, c...]
where the time goes in v4:
time: 191 us
  Pallas kernels  179 us (94%)
  local copies, waits for them, and re-layouts  11.6 us (6%)
    pallas_call x1, Pallas kernels, shards(): pl.pallas_call(layer_kernel, out_shape=(sds((rows, cols), F32), sds((8, c...  179 us
    unnamed x8, local copies, waits for them, and re-layouts  10.4 us

profile of v4, /device:TPU:1, one launch (start us, length us, event | category | flops | bytes accessed | tf_op | source)
XLA Modules:
  0.0 191.0 jit_solution(17018443188946726485)
XLA Ops:
  0.6 1.3 broadcast_in_dim.3.gain
  1.9 178.7 %shard_map.129 = (f32[128,768]{1,0:T(8,128)}, bf16[8,768,256]{2,1,0:T(8,128)(2,1)}, bf16[8,768,256]{2,1,0:T(8,128)(2,1)}, bf16[8,256,768]{2,1,0:T(8,128)(2,1)}) custom-call(bf16[128,768]{1,0:T(8,128)(2,1)} %att.1, bf16[768,384]{1,0:T(8,128)(2,1)} %op.1, bf16[128,768]{1,0:T(8,128)(2,1)} %res.1, bf16[1,768]{1,0:T(2,128)(2,1)} %broadcast_in_dim.3.gain, ...), custom_call_target="tpu_custom_call" | custom-call | flops 30000001024 | bytes 25000000 | tf_op jit(solution)/shard_map/pallas_call | solution.py:656
  180.6 1.8 copy.18
  182.4 0.0 copy-start.1
  182.4 3.9 %copy.19 = bf16[1,6144,256]{2,1,0:T(8,128)(2,1)} copy(bf16[1,6144,256]{2,1,0:T(8,128)(2,1)} %bitcast.10) | data formatting | bytes 6291456
  186.3 0.0 copy-done.1
  186.3 0.0 copy-start
  186.3 1.7 copy.20
  187.9 1.4 copy-done
  189.3 1.7 copy.21
Async XLA Ops:
  182.4 3.9 %copy-start.1 = (bf16[8,768,256]{2,1,0:T(8,128)(2,1)S(1)}, bf16[8,768,256]{2,1,0:T(8,128)(2,1)}, u32[]{:S(2)}) copy-start(bf16[8,768,256]{2,1,0:T(8,128)(2,1)} %get-tuple-element.10) | copy-start | bytes 9437188
  186.3 3.0 %copy-start = (bf16[8,256,768]{2,1,0:T(8,128)(2,1)S(1)}, bf16[8,256,768]{2,1,0:T(8,128)(2,1)}, u32[]{:S(2)}) copy-start(bf16[8,256,768]{2,1,0:T(8,128)(2,1)} %get-tuple-element.11) | copy-start | bytes 9437188
